TPU v7x, 32 devices: a whole 2x2x4 slice. The times are simulated.
32 devices in a mesh: dp: 8 (over z, core), tensor: 4 (over y, x).
Axes of the slice: x: 2, y: 2, z: 4, core: 2. Of those that a mesh axis runs over, the one named last changes fastest.
Arguments:
- x_quant: bfloat16 [96, 8192], P('tensor', 'dp'), may hold values from -6 to 6
- x_scale: float32 [4, 64], P('tensor', 'dp'), may hold values from 0.25 to 4
- x_outlier: int32 [4, 64], P('tensor', 'dp'), may hold values 0 or 1
- x_correction: bfloat16 [96, 8192], P('tensor', 'dp'), may hold values from -12 to 12
- g_quant: bfloat16 [96, 8192], P('tensor', 'dp'), may hold values from -6 to 6
- g_scale: float32 [4, 64], P('tensor', 'dp'), may hold values from 0.25 to 4
- g_outlier: int32 [4, 64], P('tensor', 'dp'), may hold values 0 or 1
- g_correction: bfloat16 [96, 8192], P('tensor', 'dp'), may hold values from -12 to 12
- gate_pre: bfloat16 [96, 26624], P('dp', 'tensor'), may hold values from -8 to 8
- up_pre: bfloat16 [96, 26624], P('dp', 'tensor'), may hold values from -6 to 6
- w_gate: bfloat16 [8192, 26624], P('dp', 'tensor'), may hold values from -0.0625 to 0.0625
- w_up: bfloat16 [8192, 26624], P('dp', 'tensor'), may hold values from -0.0625 to 0.0625
- w_down: bfloat16 [26624, 8192], P('tensor', 'dp'), may hold values from -0.0625 to 0.0625
Outputs:
- grad_input: bfloat16 [96, 8192], P('tensor', 'dp')
- grad_gate_weight: bfloat16 [8192, 26624], P('dp', 'tensor')
- grad_up_weight: bfloat16 [8192, 26624], P('dp', 'tensor')
- grad_down_weight: bfloat16 [26624, 8192], P('tensor', 'dp')
All inputs are finite; a program needn't handle non-finite values. No bound on the sum of `x_outlier` or of `g_outlier` on one device may be relied on, other than what follows from the above.
Results may differ from a plain program's by a relative error of at most 0.0064.
Values may be sent and summed in bfloat16 or wider, within the bound.
No kernel may reach another device: no remote copies, remote signals or barrier semaphores. Data moves between devices by JAX's collectives and lax.ppermute only.
A program may use at most 128 MiB of HBM per device.

v0:
```python
import jax
import jax.numpy as jnp
from jax import lax
from jax.sharding import PartitionSpec as P

BLK_C = 128


def dequantize(quant, block_scale, outlier, correction):
    scale_cols = jnp.repeat(block_scale, BLK_C, axis=1)
    outlier_cols = jnp.repeat(outlier.astype(jnp.float32), BLK_C, axis=1)
    values = scale_cols * quant.astype(jnp.float32) + outlier_cols * correction.astype(jnp.float32)
    return values.astype(jnp.bfloat16)


def contract_rows(left, right):
    return lax.dot_general(
        left, right, (((0,), (0,)), ((), ())), preferred_element_type=jnp.float32
    )


def contract_cols(left, right):
    return lax.dot_general(
        left, right, (((1,), (1,)), ((), ())), preferred_element_type=jnp.float32
    )


def on_device(
    x_quant,
    x_scale,
    x_outlier,
    x_correction,
    g_quant,
    g_scale,
    g_outlier,
    g_correction,
    gate_pre,
    up_pre,
    w_gate,
    w_up,
    w_down,
):
    inputs = dequantize(x_quant, x_scale, x_outlier, x_correction)
    out_grad = dequantize(g_quant, g_scale, g_outlier, g_correction)
    inputs_all, out_grad_all = (
        lax.all_gather(inputs, "tensor", axis=0, tiled=True),
        lax.all_gather(out_grad, "tensor", axis=0, tiled=True),
    )
    grad_rows = out_grad_all
    hidden_grad = lax.psum_scatter(
        contract_cols(grad_rows, w_down), "dp", scatter_dimension=0, tiled=True
    )
    gate_val = gate_pre.astype(jnp.float32)
    up_val = up_pre.astype(jnp.float32)
    sigmoid_gate = jax.nn.sigmoid(gate_val)
    silu_gate = gate_val * sigmoid_gate
    up_grad = (hidden_grad * silu_gate).astype(jnp.bfloat16)
    gate_grad = (
        hidden_grad * up_val * sigmoid_gate * (1.0 + gate_val * (1.0 - sigmoid_gate))
    ).astype(jnp.bfloat16)
    gate_rows = lax.all_gather(gate_pre, "dp", axis=0, tiled=True).astype(jnp.float32)
    rebuilt = (
        gate_rows
        * jax.nn.sigmoid(gate_rows)
        * lax.all_gather(up_pre, "dp", axis=0, tiled=True).astype(jnp.float32)
    ).astype(jnp.bfloat16)
    gate_piece = lax.all_gather(gate_grad, "dp", axis=0, tiled=True)
    up_piece = lax.all_gather(up_grad, "dp", axis=0, tiled=True)
    grad_rows = out_grad_all
    down_total = contract_rows(rebuilt, grad_rows)
    gate_total = contract_rows(inputs_all, gate_piece)
    up_total = contract_rows(inputs_all, up_piece)
    input_part = contract_cols(gate_piece, w_gate) + contract_cols(up_piece, w_up)
    grad_input = lax.psum_scatter(input_part, "tensor", scatter_dimension=0, tiled=True).astype(
        jnp.bfloat16
    )
    return (
        grad_input,
        gate_total.astype(jnp.bfloat16),
        up_total.astype(jnp.bfloat16),
        down_total.astype(jnp.bfloat16),
    )


def solution(mesh):
    return jax.shard_map(
        on_device,
        mesh=mesh,
        in_specs=(
            P("tensor", "dp"),
            P("tensor", "dp"),
            P("tensor", "dp"),
            P("tensor", "dp"),
            P("tensor", "dp"),
            P("tensor", "dp"),
            P("tensor", "dp"),
            P("tensor", "dp"),
            P("dp", "tensor"),
            P("dp", "tensor"),
            P("dp", "tensor"),
            P("dp", "tensor"),
            P("tensor", "dp"),
        ),
        out_specs=(P("tensor", "dp"), P("dp", "tensor"), P("dp", "tensor"), P("tensor", "dp")),
        check_vma=False,
    )
```

profile of v0, /device:TPU:0, one launch (start us, length us, event | category | flops | bytes accessed | tf_op | source)
XLA Modules:
  0.0 199.5 jit_solution(6184114559873978164)
XLA Ops:
  9.4 0.7 broadcast_bitcast_fusion.2
  10.1 0.8 add_convert_fusion.1
  10.9 10.2 %all_gather.18 = bf16[96,1024]{1,0:T(8,128)(2,1)S(1)} all-gather(bf16[24,1024]{1,0:T(8,128)(2,1)S(1)} %add_convert_fusion.1), channel_id=1, replica_groups=mesh['dp'=8,'tensor'=4] {'tensor'}, dimensions={0}, use_global_device_ids=true | all-gather | bytes 245760 | tf_op jit(solution)/shard_map/all_gather | solution.py:47
  21.1 9.2 %fusion.13 = f32[96,6656]{1,0:T(8,128)S(1)} fusion(bf16[96,1024]{1,0:T(8,128)(2,1)S(1)} %all_gather.18, bf16[6656,1024]{1,0:T(8,128)(2,1)} %param.25), kind=kOutput, calls=%fused_computation.28 | convolution fusion | flops 1308622848 | bytes 16384000 | tf_op jit(solution)/shard_map/dot_general | solution.py:23
  30.3 53.5 %fusion = f32[16,6656]{1,0:T(8,128)S(1)} fusion(f32[96,6656]{1,0:T(8,128)S(1)} %fusion.13), kind=kCustom, calls=%all-reduce-scatter | all-reduce-scatter fusion | flops 851969 | bytes 2982400
  83.9 1.4 collective-permute-start
  85.4 1.3 collective-permute-start.1
  88.0 9.0 %collective-permute-done.1 = f32[12,6656]{1,0:T(8,128)S(1)} collective-permute-done((f32[12,6656]{1,0:T(8,128)S(1)}, f32[12,6656]{1,0:T(8,128)S(1)}, u32[]{:S(2)}, u32[]{:S(2)}) %collective-permute-start.1) | collective-permute-done | bytes 319520
  97.0 1.1 concatenate
  98.1 1.0 fusion.10
  99.8 9.2 %all_gather.21 = bf16[96,1024]{1,0:T(8,128)(2,1)S(1)} all-gather(bf16[24,1024]{1,0:T(8,128)(2,1)S(1)} %add_convert_fusion), channel_id=1, replica_groups=mesh['dp'=8,'tensor'=4] {'tensor'}, dimensions={0}, use_global_device_ids=true | all-gather | bytes 245760 | tf_op jit(solution)/shard_map/all_gather | solution.py:46
  109.0 1.6 reshape.36
  110.7 2.8 %reshape.37 = f32[96,6656]{1,0:T(8,128)} reshape(bf16[8,12,6656]{2,1,0:T(8,128)(2,1)} %all-gather.15.cloned.1.call-done) | data formatting | bytes 3833856 | tf_op jit(solution)/shard_map/convert_element_type | solution.py:65
  113.5 8.8 %convolution_convert_fusion = bf16[6656,1024]{1,0:T(8,128)(2,1)} fusion(bf16[96,1024]{1,0:T(8,128)(2,1)S(1)} %all_gather.18, f32[96,6656]{1,0:T(8,128)} %reshape.37, f32[96,6656]{1,0:T(8,128)S(1)} %reshape.36), kind=kOutput, calls=%fused_computation | convolution fusion | flops 1319272448 | bytes 18939904 | tf_op jit(solution)/shard_map/dot_general | solution.py:17
  122.3 6.1 %all-gather.9.cloned.1.call-done = bf16[8,12,6656]{2,1,0:T(8,128)(2,1)} async-done(((bf16[1,12,6656]{2,1,0:T(8,128)(2,1)}), bf16[8,12,6656]{2,1,0:T(8,128)(2,1)}) %all-gather.9.cloned.1.call-update) | async-done | bytes 1277968 | tf_op jit(solution)/shard_map/all_gather | solution.py:67
  128.4 1.6 reshape.29
  130.0 9.1 %fusion.14 = f32[96,1024]{1,0:T(8,128)S(1)} fusion(bf16[96,6656]{1,0:T(8,128)(2,1)S(1)} %reshape.29, bf16[1024,6656]{1,0:T(8,128)(2,1)} %param.23), kind=kOutput, calls=%fused_computation.29 | convolution fusion | flops 1308622848 | bytes 15302656 | tf_op jit(solution)/shard_map/dot_general | solution.py:23
  139.0 16.8 %all-gather.11.cloned.1.call-done = bf16[8,12,6656]{2,1,0:T(8,128)(2,1)} async-done(((bf16[1,12,6656]{2,1,0:T(8,128)(2,1)}), bf16[8,12,6656]{2,1,0:T(8,128)(2,1)}) %all-gather.11.cloned.1.call-update) | async-done | bytes 1277968 | tf_op jit(solution)/shard_map/all_gather | solution.py:68
  155.9 1.6 reshape.31
  157.5 9.8 %convolution_add_fusion = f32[96,1024]{1,0:T(8,128)} fusion(f32[96,1024]{1,0:T(8,128)S(1)} %fusion.14, bf16[96,6656]{1,0:T(8,128)(2,1)S(1)} %reshape.31, bf16[1024,6656]{1,0:T(8,128)(2,1)} %param.24), kind=kOutput, calls=%fused_computation.5 | convolution fusion | flops 1308721152 | bytes 15695872 | tf_op jit(solution)/shard_map/dot_general | solution.py:23
  167.3 7.1 %convolution_convert_fusion.1 = bf16[1024,6656]{1,0:T(8,128)(2,1)} fusion(bf16[96,1024]{1,0:T(8,128)(2,1)S(1)} %all_gather.21, bf16[96,6656]{1,0:T(8,128)(2,1)S(1)} %reshape.31), kind=kOutput, calls=%fused_computation.1 | convolution fusion | flops 1315438592 | bytes 15106048 | tf_op jit(solution)/shard_map/dot_general | solution.py:17
  174.4 7.1 %convolution_convert_fusion.2 = bf16[1024,6656]{1,0:T(8,128)(2,1)} fusion(bf16[96,1024]{1,0:T(8,128)(2,1)S(1)} %all_gather.21, bf16[96,6656]{1,0:T(8,128)(2,1)S(1)} %reshape.29), kind=kOutput, calls=%fused_computation.2 | convolution fusion | flops 1315438592 | bytes 15106048 | tf_op jit(solution)/shard_map/dot_general | solution.py:17
  181.5 9.9 %reduce-scatter.6.cloned.1.call-done = f32[24,1024]{1,0:T(8,128)} async-done(((f32[96,1024]{1,0:T(8,128)}), f32[24,1024]{1,0:T(8,128)}) %reduce-scatter.6.cloned.1.call-update) | async-done | bytes 98320
  191.4 1.5 convert_element_type.70
  (33 shorter events, 3.5 us)
Async XLA Ops:
  7.2 101.9 %all-gather.13.cloned.1.call-start = ((), (), s32[]{:S(2)}) async-start(), calls=%async_computation.3 | async-start | bytes 1916928 | tf_op jit(solution)/shard_map/all_gather | solution.py:61
  7.9 102.8 %all-gather.15.cloned.1.call-start = ((), (), s32[]{:S(2)}) async-start(), calls=%async_computation.4 | async-start | bytes 1916928 | tf_op jit(solution)/shard_map/all_gather | solution.py:65
  8.6 119.7 %all-gather.9.cloned.1.call-start = ((), (), s32[]{:S(2)}) async-start(), calls=%async_computation.1 | async-start | bytes 1916928 | tf_op jit(solution)/shard_map/all_gather | solution.py:67
  30.3 56.5 %copy-start.5 = (u32[32]{0:T(128)S(1)}, u32[32]{0:T(128)}, u32[]{:S(2)}) copy-start(u32[32]{0:T(128)} %constant.11) | copy-start | bytes 388
  30.3 67.8 %copy-start = (bf16[12,6656]{1,0:T(8,128)(2,1)S(1)}, bf16[12,6656]{1,0:T(8,128)(2,1)}, u32[]{:S(2)}) copy-start(bf16[12,6656]{1,0:T(8,128)(2,1)} %param.21) | copy-start | bytes 479236
  83.8 14.2 %copy-start.1 = (bf16[12,6656]{1,0:T(8,128)(2,1)S(1)}, bf16[12,6656]{1,0:T(8,128)(2,1)}, u32[]{:S(2)}) copy-start(bf16[12,6656]{1,0:T(8,128)(2,1)} %param.22) | copy-start | bytes 479236
  83.9 15.3 %copy-start.6 = (s32[1,8]{1,0:T(1,128)S(1)}, s32[1,8]{1,0:T(1,128)}, u32[]{:S(2)}) copy-start(s32[1,8]{1,0:T(1,128)} %param.15) | copy-start | bytes 100
  83.9 15.3 %copy-start.4 = (f32[1,8]{1,0:T(1,128)S(1)}, f32[1,8]{1,0:T(1,128)}, u32[]{:S(2)}) copy-start(f32[1,8]{1,0:T(1,128)} %param.14) | copy-start | bytes 100
  83.9 15.9 %copy-start.2 = (bf16[24,1024]{1,0:T(8,128)(2,1)S(1)}, bf16[24,1024]{1,0:T(8,128)(2,1)}, u32[]{:S(2)}) copy-start(bf16[24,1024]{1,0:T(8,128)(2,1)} %param.16) | copy-start | bytes 147460
  83.9 15.9 %copy-start.3 = (bf16[24,1024]{1,0:T(8,128)(2,1)S(1)}, bf16[24,1024]{1,0:T(8,128)(2,1)}, u32[]{:S(2)}) copy-start(bf16[24,1024]{1,0:T(8,128)(2,1)} %param.13) | copy-start | bytes 147460
  83.9 13.1 %collective-permute-start = (f32[16,6656]{1,0:T(8,128)S(1)}, f32[16,6656]{1,0:T(8,128)S(1)}, u32[]{:S(2)}, u32[]{:S(2)}) collective-permute-start(f32[16,6656]{1,0:T(8,128)S(1)} %fusion), channel_id=1, source_target_pairs={{0,4},{4,8},{8,12},{12,16},{16,20},{20,24},{24,28},{1,5},{5,9},{9,... | collective-permute-start | bytes 1277960
  85.4 11.6 %collective-permute-start.1 = (f32[12,6656]{1,0:T(8,128)S(1)}, f32[12,6656]{1,0:T(8,128)S(1)}, u32[]{:S(2)}, u32[]{:S(2)}) collective-permute-start(f32[12,6656]{1,0:T(8,128)S(1)} %slice), channel_id=1, source_target_pairs={{0,8},{4,12},{8,16},{12,20},{16,24},{20,28},{1,9},{5,13},{9,17},{1... | collective-permute-start | bytes 958472
  99.1 56.8 %all-gather.11.cloned.1.call-start = ((), (), s32[]{:S(2)}) async-start(), calls=%async_computation.2 | async-start | bytes 1916928 | tf_op jit(solution)/shard_map/all_gather | solution.py:68
  99.7 91.7 %reduce-scatter.6.cloned.1.call-start = ((), (), s32[]{:S(2)}) async-start(), calls=%async_computation.5 | async-start | bytes 491520
Sparse Core Ops, SparseCore 0:
  9.6 28.5 all-gather.12
  39.9 36.3 all-gather.14
  99.2 29.0 all-gather.8
  130.4 25.3 all-gather.10
  167.4 23.9 reduce-scatter.5
where the time goes:
time: 200 us; the launch traced here: 199 us
  blocking collectives  73 us (36%)
  matrix products  51.1 us (26%)
  waiting for transfers between devices  43.7 us (22%)
  between operations  14.6 us (7%)
  local copies, waits for them, and re-layouts  10.1 us (5%)
  other arithmetic  4.06 us (2%)
  starting transfers between devices  2.96 us (1%)
    unnamed x1, blocking collectives  53.5 us
    dot_general x3, matrix products, contract_cols(): lax.dot_general(left, right, (((1,), (1,)), ((), ())), preferred_element_...  28 us
    dot_general x3, matrix products, contract_rows(): lax.dot_general(left, right, (((0,), (0,)), ((), ())), preferred_element_...  23 us
    unnamed x8, waiting for transfers between devices  20.7 us
    all_gather x1, waiting for transfers between devices, on_device(): up_piece = lax.all_gather(up_grad, 'dp', axis=0, tiled=True)  16.8 us
    all_gather x1, blocking collectives, on_device(): lax.all_gather(out_grad, 'tensor', axis=0, tiled=True)  10.2 us
    all_gather x1, blocking collectives, on_device(): lax.all_gather(inputs, 'tensor', axis=0, tiled=True)  9.25 us
    all_gather x1, waiting for transfers between devices, on_device(): gate_piece = lax.all_gather(gate_grad, 'dp', axis=0, tiled=True)  6.07 us
  transfers between devices with their start and end apart: 7, of which 4 were waited for; matrix products, arithmetic and copies ran while one was open for 53% of the time, Pallas kernels for 0%

commit v1 on v0

v1 whole, which is shorter than its diff:
```python
import functools

import jax
import jax.numpy as jnp
from jax import lax
from jax.experimental import pallas as pl
from jax.experimental.pallas import tpu as pltpu
from jax.sharding import PartitionSpec as P

BLK_C = 128
F32 = jnp.float32
BF16 = jnp.bfloat16
VMEM = pltpu.VMEM
SMEM = pltpu.SMEM


def whole(space=VMEM):
    return pl.BlockSpec(memory_space=space)


def shape(dims, dtype):
    return jax.ShapeDtypeStruct(dims, dtype)


def params(mib=56):
    return pltpu.CompilerParams(vmem_limit_bytes=mib * 1024 * 1024)


def cost(flops, nbytes):
    return pl.CostEstimate(flops=int(flops), bytes_accessed=int(nbytes), transcendentals=0)


def tile_of(extent):
    return next(t for t in (512, 256, 128) if extent % t == 0)


def pieces(extent, step):
    return [(at, min(step, extent - at)) for at in range(0, extent, step)]


def prep_kernel(xq, xs, xo, xc, gq, gs, go, gc, gate, up, xg, gu):
    for at, (quant, scale, flag, corr) in enumerate(((gq, gs, go, gc), (xq, xs, xo, xc))):
        for b in range(scale.shape[1]):
            cols = slice(b * BLK_C, (b + 1) * BLK_C)
            value = scale[0, b] * quant[:, cols].astype(F32) + flag[0, b].astype(F32) * corr[
                :, cols
            ].astype(F32)
            xg[at, :, cols] = value.astype(BF16)
    gu[...] = jnp.concatenate([gate[...].astype(F32), up[...].astype(F32)], 0).astype(BF16)


def prep(xq, xs, xo, xc, gq, gs, go, gc, gate, up):
    rows, width = xq.shape
    tok, ff = gate.shape
    return pl.pallas_call(
        prep_kernel,
        out_shape=(shape((2, rows, width), BF16), shape((2 * tok, ff), BF16)),
        in_specs=[whole(), whole(SMEM), whole(SMEM), whole()] * 2 + [whole()] * 2,
        out_specs=(whole(), whole()),
        compiler_params=params(),
        cost_estimate=cost(0, 4 * xq.size * 2 + gate.size * 8),
    )(xq, xs, xo, xc, gq, gs, go, gc, gate, up)


def load_down(place, half, width, w_hbm, w_vmem, sems):
    copies = []
    for k, (at, size) in enumerate(pieces(width, 256)):
        start = pl.multiple_of(half + at, 16)
        copy = pltpu.make_async_copy(
            w_hbm.at[pl.ds(start, size)], w_vmem.at[pl.ds(at, size)], sems.at[k]
        )
        copy.start()
        copies.append(copy)
    return copies


def hidden_half(copies, grads, width, w_vmem, out):
    groups, rows = out.shape[0], out.shape[1]
    for copy, (at, size) in zip(copies, pieces(width, 256)):
        copy.wait()
        total = lax.dot_general(
            grads, w_vmem[at : at + size, :], (((1,), (1,)), ((), ())), preferred_element_type=F32
        )
        for q in range(groups):
            out[q, :, at : at + size] = total[q * rows : (q + 1) * rows, :].astype(out.dtype)


def first_half_kernel(n_t, offset, place, *refs):
    parts, (w_hbm, grads_out, inputs_t, out, w_vmem, held, sems) = refs[:n_t], refs[n_t:]
    core, me = place[0], place[2]
    width = out.shape[2]
    copies = load_down(place, (1 - core) * offset, width, w_hbm, w_vmem, sems)
    rows = held.shape[1]
    for s in range(n_t):
        held[me ^ s] = parts[s][1].astype(F32)
    inputs = held[...].reshape(n_t * rows, held.shape[2])
    inputs_t[...] = inputs.T.astype(BF16)
    for s in range(n_t):
        held[me ^ s] = parts[s][0].astype(F32)
    grads = held[...].reshape(n_t * rows, held.shape[2]).astype(BF16)
    grads_out[...] = grads
    hidden_half(copies, grads, width, w_vmem, out)


def second_half_kernel(offset, place, grads, w_hbm, out, w_vmem, sems):
    width = out.shape[2]
    copies = load_down(place, place[0] * offset, width, w_hbm, w_vmem, sems)
    hidden_half(copies, grads[...], width, w_vmem, out)


def first_half(place, parts, w_down, n_z, width):
    n_t, rows, chans = len(parts), parts[0].shape[1], parts[0].shape[2]
    tokens = n_t * rows
    n_copies = len(pieces(width, 256))
    return pl.pallas_call(
        functools.partial(first_half_kernel, n_t, w_down.shape[0] - width),
        out_shape=(
            shape((tokens, chans), BF16),
            shape((chans, tokens), BF16),
            shape((n_z, tokens // n_z, width), BF16),
        ),
        in_specs=[whole(SMEM)] + [whole()] * n_t + [whole(pl.ANY)],
        out_specs=(whole(), whole(), whole()),
        scratch_shapes=[
            VMEM((width, chans), BF16),
            VMEM((n_t, rows, chans), F32),
            pltpu.SemaphoreType.DMA((n_copies,)),
        ],
        compiler_params=params(),
        cost_estimate=cost(2 * tokens * chans * width, 2 * chans * width),
    )(place, *parts, w_down)


def second_half(place, grads, w_down, n_z, width):
    tokens, chans = grads.shape
    n_copies = len(pieces(width, 256))
    return pl.pallas_call(
        functools.partial(second_half_kernel, w_down.shape[0] - width),
        out_shape=shape((n_z, tokens // n_z, width), F32),
        in_specs=[whole(SMEM), whole(), whole(pl.ANY)],
        out_specs=whole(),
        scratch_shapes=[VMEM((width, chans), BF16), pltpu.SemaphoreType.DMA((n_copies,))],
        compiler_params=params(),
        cost_estimate=cost(2 * tokens * chans * width, 2 * chans * width),
    )(place, grads, w_down)


def pair_kernel(picks, place, mine, theirs, own, *outs):
    z, n_z = place[1], mine.shape[0]

    def chunk(at):
        return mine[at] + theirs[at].astype(F32)

    own[...] = chunk(z)
    for pick, out in zip(picks, outs):
        out[...] = chunk(pick(z, n_z)).astype(out.dtype)


def pair_sum(place, mine, theirs, picks):
    n_z, rows, width = mine.shape
    return pl.pallas_call(
        functools.partial(pair_kernel, picks),
        out_shape=(shape((rows, width), F32),) + (shape((rows, width), BF16),) * len(picks),
        in_specs=[whole(SMEM), whole(), whole()],
        out_specs=(whole(),) * (1 + len(picks)),
        compiler_params=params(),
        cost_estimate=cost(0, mine.size * 12),
    )(place, mine, theirs)


def add_kernel(*refs):
    *terms, out = refs
    total = terms[0][...].astype(F32)
    for term in terms[1:]:
        total = total + term[...].astype(F32)
    out[...] = total.astype(out.dtype)


def add_all(*terms):
    return pl.pallas_call(
        add_kernel,
        out_shape=shape(terms[0].shape, BF16),
        in_specs=[whole()] * len(terms),
        out_specs=whole(),
        compiler_params=params(),
        cost_estimate=cost(0, terms[0].size * 2 * (len(terms) + 2)),
    )(*terms)


def z_pairs(pairs):
    return [(2 * a + c, 2 * b + c) for a, b in pairs for c in range(2)]


def z_shift(value, pairs):
    return lax.ppermute(value, "dp", z_pairs(pairs))


def swap_cores(value, n_z):
    return lax.ppermute(value, "dp", [(2 * z + c, 2 * z + 1 - c) for z in range(n_z) for c in range(2)])


LINE = 4
RIGHT = [(0, 1), (1, 2), (2, 3)]
LEFT = [(1, 0), (2, 1), (3, 2)]
ACROSS = [(0, 2), (1, 3), (2, 0), (3, 1)]


def gather_kernel(n_z, place, own, *refs):
    *parts, out = refs
    z = place[1]
    out[z] = own[...]
    if n_z == LINE:
        right, left, across, far = parts
        out[z ^ 2] = across[...]

        @pl.when(z == 0)
        def _():
            out[1] = left[...]
            out[3] = far[...]

        @pl.when(z == n_z - 1)
        def _():
            out[2] = right[...]
            out[0] = far[...]

        @pl.when((z > 0) & (z < n_z - 1))
        def _():
            out[z - 1] = right[...]
            out[z + 1] = left[...]

    else:
        for s, part in enumerate(parts, 1):
            out[lax.rem(z + n_z - s, n_z)] = part[...]


def gather_z(place, own, n_z):
    if n_z == LINE:
        across = z_shift(own, ACROSS)
        parts = [z_shift(own, RIGHT), z_shift(own, LEFT), across, z_shift(across, [(2, 3), (1, 0)])]
    else:
        parts = [
            z_shift(own, [(a, (a + s) % n_z) for a in range(n_z)]) for s in range(1, n_z)
        ]
    return pl.pallas_call(
        functools.partial(gather_kernel, n_z),
        out_shape=shape((n_z,) + own.shape, own.dtype),
        in_specs=[whole(SMEM)] + [whole()] * (1 + len(parts)),
        out_specs=whole(),
        compiler_params=params(),
        cost_estimate=cost(0, own.size * 2 * 2 * n_z),
    )(place, own, *parts)


def reduce_z(place, mine, theirs):
    n_z = mine.shape[0]
    if n_z == LINE:
        picks = (
            lambda z, n: lax.rem(z + 1, n),
            lambda z, n: lax.rem(z + n - 1, n),
            lambda z, n: z ^ 2,
            lambda z, n: jnp.where(z == 0, n - 1, 0),
        )
        own, right, left, across, far = pair_sum(place, mine, theirs, picks)
        from_far = z_shift(far, [(3, 2), (0, 1)])
        from_left = z_shift(right, RIGHT)
        from_right = z_shift(left, LEFT)
        from_across = z_shift(add_all(across, from_far), ACROSS)
        return add_all(own, from_left, from_right, from_across)
    picks = tuple(lambda z, n, s=s: lax.rem(z + s, n) for s in range(1, n_z))
    own, *sends = pair_sum(place, mine, theirs, picks)
    got = [
        z_shift(part, [(a, (a + s) % n_z) for a in range(n_z)]) for s, part in enumerate(sends, 1)
    ]
    return add_all(own, *got)


def down_kernel(place, mine, theirs, grads, out, gate_factor, up_factor):
    core0 = place[0] == 0
    n_z, double, _ = mine.shape
    tok = double // 2
    gate, up = [], []
    for q in range(n_z):
        a, b = mine[q].astype(F32), theirs[q].astype(F32)
        first, second = jnp.where(core0, a, b), jnp.where(core0, b, a)
        gate += [first[:tok], second[:tok]]
        up += [first[tok:], second[tok:]]
    gate, up = jnp.concatenate(gate, 0), jnp.concatenate(up, 0)
    sig = 1.0 / (1.0 + jnp.exp(-gate))
    silu = gate * sig
    hidden = (silu * up).astype(BF16)
    gate_factor[...] = up * sig * (1.0 + gate * (1.0 - sig))
    up_factor[...] = silu
    out[...] = lax.dot_general(
        hidden, grads[...], (((0,), (0,)), ((), ())), preferred_element_type=F32
    ).astype(BF16)


def down_grad(place, mine, theirs, grads):
    n_z, double, ff = mine.shape
    tokens, chans = grads.shape
    t = tile_of(ff)
    rows = pl.BlockSpec((n_z, double, t), lambda i: (0, 0, i))
    cols = pl.BlockSpec((tokens, t), lambda i: (0, i))
    return pl.pallas_call(
        down_kernel,
        grid=(ff // t,),
        out_shape=(shape((ff, chans), BF16), shape((tokens, ff), F32), shape((tokens, ff), F32)),
        in_specs=[whole(SMEM), rows, rows, pl.BlockSpec((tokens, chans), lambda i: (0, 0))],
        out_specs=(pl.BlockSpec((t, chans), lambda i: (i, 0)), cols, cols),
        compiler_params=params(),
        cost_estimate=cost(2 * tokens * chans * ff, 2 * chans * ff + 8 * tokens * ff),
    )(place, mine, theirs, grads)


def input_kernel(n_t, place, mine, theirs, gate_factor, up_factor, w_gate, w_up, *refs):
    (gate_grad, up_grad), pieces_out, (hidden_grad, total) = refs[:2], refs[2 : 2 + n_t], refs[2 + n_t :]
    i, steps = pl.program_id(0), pl.num_programs(0)
    n_z, rows, width = mine.shape
    t = gate_grad.shape[1]

    @pl.when(i == 0)
    def _():
        core0 = place[0] == 0
        ff = hidden_grad.shape[0] * t
        low = ff - width
        for q in range(n_z):
            a, b = mine[q].astype(F32), theirs[q].astype(F32)
            line = jnp.concatenate([jnp.where(core0, a, b)[:, :low], jnp.where(core0, b, a)], 1)
            for k in range(ff // t):
                hidden_grad[k, q * rows : (q + 1) * rows, :] = line[:, k * t : (k + 1) * t]
        total[...] = jnp.zeros_like(total)

    hidden = hidden_grad[i]
    gate = (hidden * gate_factor[...]).astype(BF16)
    up = (hidden * up_factor[...]).astype(BF16)
    gate_grad[...] = gate
    up_grad[...] = up
    dims = (((1,), (1,)), ((), ()))
    term = lax.dot_general(gate, w_gate[...], dims, preferred_element_type=F32)
    term += lax.dot_general(up, w_up[...], dims, preferred_element_type=F32)
    total[...] += term.reshape(total.shape)

    @pl.when(i == steps - 1)
    def _():
        for s, out in enumerate(pieces_out):
            out[...] = total[place[2] ^ s].astype(out.dtype)


def input_grad(place, mine, theirs, gate_factor, up_factor, w_gate, w_up, n_t):
    tokens, ff = gate_factor.shape
    chans = w_gate.shape[0]
    t = tile_of(ff)
    rows = tokens // n_t
    cols = pl.BlockSpec((tokens, t), lambda i: (0, i))
    weight = pl.BlockSpec((chans, t), lambda i: (0, i))
    held = pl.BlockSpec(mine.shape, lambda i: (0, 0, 0))
    piece = pl.BlockSpec((rows, chans), lambda i: (0, 0))
    return pl.pallas_call(
        functools.partial(input_kernel, n_t),
        grid=(ff // t,),
        out_shape=(shape((tokens, ff), BF16),) * 2
        + (shape((rows, chans), F32),)
        + (shape((rows, chans), BF16),) * (n_t - 1),
        in_specs=[whole(SMEM), held, held, cols, cols, weight, weight],
        out_specs=(cols, cols) + (piece,) * n_t,
        scratch_shapes=[VMEM((ff // t, tokens, t), F32), VMEM((n_t, rows, chans), F32)],
        compiler_params=params(),
        cost_estimate=cost(4 * tokens * chans * ff, 4 * chans * ff + 12 * tokens * ff),
    )(place, mine, theirs, gate_factor, up_factor, w_gate, w_up)


def weight_kernel(inputs_t, gate_grad, up_grad, gate_out, up_out):
    for grad, out in ((gate_grad, gate_out), (up_grad, up_out)):
        out[...] = lax.dot_general(
            inputs_t[...], grad[...], (((1,), (0,)), ((), ())), preferred_element_type=F32
        ).astype(BF16)


def weight_grads(inputs_t, gate_grad, up_grad):
    chans, tokens = inputs_t.shape
    ff = gate_grad.shape[1]
    t = tile_of(ff)
    cols = pl.BlockSpec((tokens, t), lambda i: (0, i))
    weight = pl.BlockSpec((chans, t), lambda i: (0, i))
    return pl.pallas_call(
        weight_kernel,
        grid=(ff // t,),
        out_shape=(shape((chans, ff), BF16),) * 2,
        in_specs=[pl.BlockSpec((chans, tokens), lambda i: (0, 0)), cols, cols],
        out_specs=(weight, weight),
        compiler_params=params(),
        cost_estimate=cost(4 * tokens * chans * ff, 4 * chans * ff + 4 * tokens * ff),
    )(inputs_t, gate_grad, up_grad)


def on_device(n_z, n_t, xq, xs, xo, xc, gq, gs, go, gc, gate_pre, up_pre, w_gate, w_up, w_down):
    dp = lax.axis_index("dp")
    place = jnp.stack([dp % 2, dp // 2, lax.axis_index("tensor")]).astype(jnp.int32)
    ff = gate_pre.shape[1]
    width = -(-ff // 256) * 128

    def to_tensor(value, s):
        return lax.ppermute(value, "tensor", [(a, a ^ s) for a in range(n_t)])

    own, gate_up = prep(xq, xs, xo, xc, gq, gs, go, gc, gate_pre, up_pre)
    parts = [own] + [to_tensor(own, s) for s in range(1, n_t)]
    gate_up = gather_z(place, gate_up, n_z)
    grads, inputs_t, send = first_half(place, parts, w_down, n_z, width)
    got = swap_cores(send, n_z)
    mine = second_half(place, grads, w_down, n_z, width)
    hidden_grad = gather_z(place, reduce_z(place, mine, got), n_z)
    grad_down, gate_factor, up_factor = down_grad(place, gate_up, swap_cores(gate_up, n_z), grads)
    gate_grad, up_grad, kept, *sends = input_grad(
        place, hidden_grad, swap_cores(hidden_grad, n_z), gate_factor, up_factor, w_gate, w_up, n_t
    )
    terms = [to_tensor(part, s) for s, part in enumerate(sends, 1)]
    grad_gate, grad_up = weight_grads(inputs_t, gate_grad, up_grad)
    return add_all(kept, *terms), grad_gate, grad_up, grad_down


def solution(mesh):
    n_z, n_t = mesh.shape["dp"] // 2, mesh.shape["tensor"]
    by_token, by_dp = P("tensor", "dp"), P("dp", "tensor")
    return jax.shard_map(
        functools.partial(on_device, n_z, n_t),
        mesh=mesh,
        in_specs=(by_token,) * 8 + (by_dp,) * 4 + (by_token,),
        out_specs=(by_token, by_dp, by_dp, by_token),
        check_vma=False,
    )
```

time: 200 us -> 159 us (0.80)
  Pallas kernels: 0 us -> 78.5 us
  blocking collectives: 73 us -> 0 us
  matrix products: 51.1 us -> 0 us
  starting transfers between devices: 2.96 us -> 37.2 us
  between operations: 14.6 us -> 0.9 us
  waiting for transfers between devices: 43.7 us -> 32.7 us
  other arithmetic: 4.06 us -> 0.61 us
  local copies, waits for them, and re-layouts: 10.1 us -> 6.99 us
    pallas_call x0 -> x12, Pallas kernels: none -> 78.5 us  [the longest x1 19.9 us: input_grad(): pl.pallas_call(functools.partial(input_kernel, n_t), grid=(ff // t,), out...]
    unnamed x1 -> x0, blocking collectives: 53.5 us -> none
    dot_general x6 -> x0, matrix products: 51.1 us -> none  [the longest x3 28 us: contract_cols(): lax.dot_general(left, right, (((1,), (1,)), ((), ())), preferred_element_...]
    ppermute x0 -> x21, starting transfers between devices: none -> 37.2 us  [the longest x12 29.1 us: z_shift(): return lax.ppermute(value, 'dp', z_pairs(pairs))]
    ppermute x0 -> x21, waiting for transfers between devices: none -> 32.7 us  [the longest x12 31.5 us: z_shift(): return lax.ppermute(value, 'dp', z_pairs(pairs))]
    all_gather x4 -> x0, waiting for transfers between devices: 22.9 us -> none  [the longest x1 16.8 us: on_device(): up_piece = lax.all_gather(up_grad, 'dp', axis=0, tiled=True)]
    unnamed x8 -> x0, waiting for transfers between devices: 20.7 us -> none
    all_gather x2 -> x0, blocking collectives: 19.4 us -> none  [the longest x1 10.2 us: on_device(): lax.all_gather(out_grad, 'tensor', axis=0, tiled=True)]
  transfers between devices with their start and end apart: 7 -> 21, of which waited for: 4 -> 10; matrix products, arithmetic and copies ran while one was open for 53% -> 0% of each run, Pallas kernels for 0% -> 35%
where the time goes in v1:
time: 159 us; the launch traced here: 157 us
  Pallas kernels  78.5 us (49%)
  starting transfers between devices  37.2 us (23%)
  waiting for transfers between devices  32.7 us (21%)
  local copies, waits for them, and re-layouts  6.99 us (4%)
    ppermute x12, waiting for transfers between devices, z_shift(): return lax.ppermute(value, 'dp', z_pairs(pairs))  31.5 us
    ppermute x12, starting transfers between devices, z_shift(): return lax.ppermute(value, 'dp', z_pairs(pairs))  29.1 us
    pallas_call x1, Pallas kernels, input_grad(): pl.pallas_call(functools.partial(input_kernel, n_t), grid=(ff // t,), out...  19.9 us
    pallas_call x1, Pallas kernels, weight_grads(): pl.pallas_call(weight_kernel, grid=(ff // t,), out_shape=(shape((chans, f...  14.3 us
    pallas_call x1, Pallas kernels, down_grad(): pl.pallas_call(down_kernel, grid=(ff // t,), out_shape=(shape((ff, chans)...  13.1 us
    pallas_call x1, Pallas kernels, second_half(): pl.pallas_call(functools.partial(second_half_kernel, w_down.shape[0] - wi...  8.46 us
    pallas_call x1, Pallas kernels, first_half(): pl.pallas_call(functools.partial(first_half_kernel, n_t, w_down.shape[0]...  8.38 us
    ppermute x6, starting transfers between devices, to_tensor(): return lax.ppermute(value, 'tensor', [(a, a ^ s) for a in range(n_t)])  8.04 us
  transfers between devices with their start and end apart: 21, of which 10 were waited for; matrix products, arithmetic and copies ran while one was open for 0% of the time, Pallas kernels for 35%

profile of v1, /device:TPU:0, one launch (start us, length us, event | category | flops | bytes accessed | tf_op | source)
XLA Modules:
  0.0 156.9 jit_solution(120561470201357874)
XLA Ops:
  0.6 2.0 %shard_map.156 = (bf16[2,24,1024]{2,1,0:T(8,128)(2,1)}, bf16[24,6656]{1,0:T(8,128)(2,1)}) custom-call(bf16[24,1024]{1,0:T(8,128)(2,1)} %xq.1, f32[1,8]{1,0:T(1,128)} %xs.1, s32[1,8]{1,0:T(1,128)} %xo.1, bf16[24,1024]{1,0:T(8,128)(2,1)} %xc.1, bf16[24,1024]{1,0:T(8,128)(2,1)} %gq.1, f32[1,8]{1,0:T(1,128)} %gs.1, s32[1,8]{1,0:T(1,128)} %go.1, ...), custom_call_target="tpu_custom_call" | custom-call | bytes 835584 | tf_op jit(solution)/shard_map/pallas_call | solution.py:55
  2.6 3.9 %collective-permute-start.2 = (bf16[2,24,1024]{2,1,0:T(8,128)(2,1)}, bf16[2,24,1024]{2,1,0:T(8,128)(2,1)S(1)}, u32[]{:S(2)}, u32[]{:S(2)}) collective-permute-start(bf16[2,24,1024]{2,1,0:T(8,128)(2,1)} %get-tuple-element.25.refs_0_), channel_id=1, source_target_pairs={{0,3},{1,2},{2,1},{3,0},{4,7},{5,6},{6,5},{7,4},{8,11},{9,10},{10,... | collective-permute-start | bytes 294920 | tf_op jit(solution)/shard_map/ppermute | solution.py:403
  7.1 3.0 %collective-permute-start.15 = (bf16[24,6656]{1,0:T(8,128)(2,1)}, bf16[24,6656]{1,0:T(8,128)(2,1)S(1)}, u32[]{:S(2)}, u32[]{:S(2)}) collective-permute-start(bf16[24,6656]{1,0:T(8,128)(2,1)} %get-tuple-element.33.own), channel_id=1, source_target_pairs={{0,16},{4,20},{8,24},{12,28},{16,0},{20,4},{24,8},{28,12},{1,17},{... | collective-permute-start | bytes 958472 | tf_op jit(solution)/shard_map/ppermute | solution.py:195
  12.9 8.4 %shard_map.157 = (bf16[96,1024]{1,0:T(8,128)(2,1)}, bf16[1024,96]{1,0:T(8,128)(2,1)}, bf16[4,24,3328]{2,1,0:T(8,128)(2,1)}) custom-call(s32[3]{0:T(128)} %pad_add_fusion.place, bf16[2,24,1024]{2,1,0:T(8,128)(2,1)} %get-tuple-element.25.refs_0_, bf16[2,24,1024]{2,1,0:T(8,128)(2,1)} %copy-done.17, bf16[2,24,1024]{2,1,0:T(8,128)(2,1)} %copy-done.16, ...), custom_call_target="tpu_custom_call" | custom-call | flops 654311424 | bytes 6815744 | tf_op jit(solution)/shard_map/pallas_call | solution.py:115
  22.7 4.6 %collective-permute-start.13 = (bf16[24,6656]{1,0:T(8,128)(2,1)S(1)}, bf16[24,6656]{1,0:T(8,128)(2,1)S(1)}, u32[]{:S(2)}, u32[]{:S(2)}) collective-permute-start(bf16[24,6656]{1,0:T(8,128)(2,1)S(1)} %copy-done.2), channel_id=1, source_target_pairs={{0,8},{4,12},{8,16},{12,20},{16,24},{20,28},{1,9},{5,13},{9,17},{1... | collective-permute-start | bytes 958472 | tf_op jit(solution)/shard_map/ppermute | solution.py:195
  28.6 5.0 %collective-permute-done.14.refs_1_ = bf16[24,6656]{1,0:T(8,128)(2,1)S(1)} collective-permute-done((bf16[24,6656]{1,0:T(8,128)(2,1)S(1)}, bf16[24,6656]{1,0:T(8,128)(2,1)S(1)}, u32[]{:S(2)}, u32[]{:S(2)}) %collective-permute-start.14) | collective-permute-done | bytes 319520 | tf_op jit(solution)/shard_map/ppermute | solution.py:195
  34.5 5.7 %collective-permute-done.16.refs_3_ = bf16[24,6656]{1,0:T(8,128)(2,1)S(1)} collective-permute-done((bf16[24,6656]{1,0:T(8,128)(2,1)S(1)}, bf16[24,6656]{1,0:T(8,128)(2,1)S(1)}, u32[]{:S(2)}, u32[]{:S(2)}) %collective-permute-start.16) | collective-permute-done | bytes 319520 | tf_op jit(solution)/shard_map/ppermute | solution.py:195
  40.9 2.6 %shard_map.163.mine = bf16[4,24,6656]{2,1,0:T(8,128)(2,1)} custom-call(s32[3]{0:T(128)} %pad_add_fusion.place, bf16[24,6656]{1,0:T(8,128)(2,1)} %get-tuple-element.33.own, bf16[24,6656]{1,0:T(8,128)(2,1)} %copy-done.5, bf16[24,6656]{1,0:T(8,128)(2,1)} %copy-done.4, bf16[24,6656]{1,0:T(8,128)(2,1)} %copy-done.3, bf16[24,6656]{1,0:T(8,128)(2,1)} %copy-done.6), custom_call_target="tpu_custom_call" | custom-call | bytes 2555904 | tf_op jit(solution)/shard_map/pallas_call | solution.py:244
  43.5 8.5 %shard_map.158.mine = f32[4,24,3328]{2,1,0:T(8,128)} custom-call(s32[3]{0:T(128)} %pad_add_fusion.place, bf16[96,1024]{1,0:T(8,128)(2,1)} %get-tuple-element.26.grads, bf16[6656,1024]{1,0:T(8,128)(2,1)} %w_hbm.1), custom_call_target="tpu_custom_call" | custom-call | flops 654311424 | bytes 6815744 | tf_op jit(solution)/shard_map/pallas_call | solution.py:137
  52.8 2.5 %shard_map.159 = (f32[24,3328]{1,0:T(8,128)}, bf16[24,3328]{1,0:T(8,128)(2,1)}, bf16[24,3328]{1,0:T(8,128)(2,1)}, bf16[24,3328]{1,0:T(8,128)(2,1)}, bf16[24,3328]{1,0:T(8,128)(2,1)}) custom-call(s32[3]{0:T(128)} %pad_add_fusion.place, f32[4,24,3328]{2,1,0:T(8,128)} %shard_map.158.mine, bf16[4,24,3328]{2,1,0:T(8,128)(2,1)} %copy-done), custom_call_target="tpu_custom_call" | custom-call | bytes 3833856 | tf_op jit(solution)/shard_map/pallas_call | solution.py:161
  59.4 2.2 %collective-permute-done.6.refs_1_ = bf16[24,3328]{1,0:T(8,128)(2,1)S(1)} collective-permute-done((bf16[24,3328]{1,0:T(8,128)(2,1)}, bf16[24,3328]{1,0:T(8,128)(2,1)S(1)}, u32[]{:S(2)}, u32[]{:S(2)}) %collective-permute-start.6) | collective-permute-done | bytes 159776 | tf_op jit(solution)/shard_map/ppermute | solution.py:195
  62.2 1.7 %shard_map.160 = bf16[24,3328]{1,0:T(8,128)(2,1)} custom-call(bf16[24,3328]{1,0:T(8,128)(2,1)} %get-tuple-element.31.refs_0_, bf16[24,3328]{1,0:T(8,128)(2,1)} %copy-done.7), custom_call_target="tpu_custom_call" | custom-call | bytes 638976 | tf_op jit(solution)/shard_map/pallas_call | solution.py:180
  63.9 6.4 %collective-permute-start.7 = (bf16[24,3328]{1,0:T(8,128)(2,1)}, bf16[24,3328]{1,0:T(8,128)(2,1)S(1)}, u32[]{:S(2)}, u32[]{:S(2)}) collective-permute-start(bf16[24,3328]{1,0:T(8,128)(2,1)} %shard_map.160), channel_id=1, source_target_pairs={{0,16},{4,20},{8,24},{12,28},{16,0},{20,4},{24,8},{28,12},{1,17},{... | collective-permute-start | bytes 479240 | tf_op jit(solution)/shard_map/ppermute | solution.py:195
  70.4 8.0 %collective-permute-done.7.refs_3_ = bf16[24,3328]{1,0:T(8,128)(2,1)S(1)} collective-permute-done((bf16[24,3328]{1,0:T(8,128)(2,1)}, bf16[24,3328]{1,0:T(8,128)(2,1)S(1)}, u32[]{:S(2)}, u32[]{:S(2)}) %collective-permute-start.7) | collective-permute-done | bytes 159776 | tf_op jit(solution)/shard_map/ppermute | solution.py:195
  79.1 1.9 %shard_map.161.own = bf16[24,3328]{1,0:T(8,128)(2,1)} custom-call(f32[24,3328]{1,0:T(8,128)} %get-tuple-element.28.refs_0_, bf16[24,3328]{1,0:T(8,128)(2,1)} %copy-done.8, bf16[24,3328]{1,0:T(8,128)(2,1)} %copy-done.9, bf16[24,3328]{1,0:T(8,128)(2,1)} %copy-done.13), custom_call_target="tpu_custom_call" | custom-call | bytes 958464 | tf_op jit(solution)/shard_map/pallas_call | solution.py:180
  82.3 5.9 %collective-permute-start.8 = (bf16[24,3328]{1,0:T(8,128)(2,1)}, bf16[24,3328]{1,0:T(8,128)(2,1)S(1)}, u32[]{:S(2)}, u32[]{:S(2)}) collective-permute-start(bf16[24,3328]{1,0:T(8,128)(2,1)} %shard_map.161.own), channel_id=1, source_target_pairs={{0,8},{4,12},{8,16},{12,20},{16,24},{20,28},{1,9},{5,13},{9,17},{1... | collective-permute-start | bytes 479240 | tf_op jit(solution)/shard_map/ppermute | solution.py:195
  88.2 3.3 %collective-permute-done.10.refs_2_ = bf16[24,3328]{1,0:T(8,128)(2,1)S(1)} collective-permute-done((bf16[24,3328]{1,0:T(8,128)(2,1)}, bf16[24,3328]{1,0:T(8,128)(2,1)S(1)}, u32[]{:S(2)}, u32[]{:S(2)}) %collective-permute-start.10) | collective-permute-done | bytes 159776 | tf_op jit(solution)/shard_map/ppermute | solution.py:195
  93.3 5.8 %collective-permute-done.11.refs_3_ = bf16[24,3328]{1,0:T(8,128)(2,1)S(1)} collective-permute-done((bf16[24,3328]{1,0:T(8,128)(2,1)S(1)}, bf16[24,3328]{1,0:T(8,128)(2,1)S(1)}, u32[]{:S(2)}, u32[]{:S(2)}) %collective-permute-start.11) | collective-permute-done | bytes 159776 | tf_op jit(solution)/shard_map/ppermute | solution.py:195
  99.8 2.1 %shard_map.162.mine = bf16[4,24,3328]{2,1,0:T(8,128)(2,1)} custom-call(s32[3]{0:T(128)} %pad_add_fusion.place, bf16[24,3328]{1,0:T(8,128)(2,1)} %shard_map.161.own, bf16[24,3328]{1,0:T(8,128)(2,1)} %copy-done.12, bf16[24,3328]{1,0:T(8,128)(2,1)} %copy-done.11, bf16[24,3328]{1,0:T(8,128)(2,1)} %copy-done.10, bf16[24,3328]{1,0:T(8,128)(2,1)} %copy-done.14), custom_call_target="tpu_custom_call" | custom-call | bytes 1277952 | tf_op jit(solution)/shard_map/pallas_call | solution.py:244
  103.0 13.1 %shard_map.164 = (bf16[6656,1024]{1,0:T(8,128)(2,1)}, f32[96,6656]{1,0:T(8,128)}, f32[96,6656]{1,0:T(8,128)}) custom-call(s32[3]{0:T(128)} %pad_add_fusion.place, bf16[4,24,6656]{2,1,0:T(8,128)(2,1)} %shard_map.163.mine, bf16[4,24,6656]{2,1,0:T(8,128)(2,1)} %copy-done.21, bf16[96,1024]{1,0:T(8,128)(2,1)} %get-tuple-element.26.grads), custom_call_target="tpu_custom_call" | custom-call | flops 1308622848 | bytes 18743296 | tf_op jit(solution)/shard_map/pallas_call | solution.py:304
  116.9 19.9 %shard_map.165 = (bf16[96,6656]{1,0:T(8,128)(2,1)}, bf16[96,6656]{1,0:T(8,128)(2,1)}, f32[24,1024]{1,0:T(8,128)}, bf16[24,1024]{1,0:T(8,128)(2,1)}, bf16[24,1024]{1,0:T(8,128)(2,1)}, /*index=5*/bf16[24,1024]{1,0:T(8,128)(2,1)}) custom-call(s32[3]{0:T(128)} %pad_add_fusion.place, bf16[4,24,3328]{2,1,0:T(8,128)(2,1)} %shard_map.162.mine, ...), custom_call_target="tpu_custom_call" | custom-call | flops 2617245696 | bytes 34930688 | tf_op jit(solution)/shard_map/pallas_call | solution.py:358
  136.8 1.5 collective-permute-start.18
  140.4 14.3 %shard_map.167 = (bf16[1024,6656]{1,0:T(8,128)(2,1)}, bf16[1024,6656]{1,0:T(8,128)(2,1)}) custom-call(bf16[1024,96]{1,0:T(8,128)(2,1)} %get-tuple-element.40.inputs_t, bf16[96,6656]{1,0:T(8,128)(2,1)} %get-tuple-element.41.gate_grad, bf16[96,6656]{1,0:T(8,128)(2,1)} %get-tuple-element.42.up_grad), custom_call_target="tpu_custom_call" | custom-call | flops 2617245696 | bytes 29818880 | tf_op jit(solution)/shard_map/pallas_call | solution.py:385
  155.4 1.6 %shard_map.166 = bf16[24,1024]{1,0:T(8,128)(2,1)} custom-call(f32[24,1024]{1,0:T(8,128)} %get-tuple-element.36.refs_0_, bf16[24,1024]{1,0:T(8,128)(2,1)} %copy-done.18, bf16[24,1024]{1,0:T(8,128)(2,1)} %copy-done.19, bf16[24,1024]{1,0:T(8,128)(2,1)} %copy-done.20), custom_call_target="tpu_custom_call" | custom-call | bytes 294912 | tf_op jit(solution)/shard_map/pallas_call | solution.py:180
  (75 shorter events, 22.2 us)
Async XLA Ops:
  2.6 8.1 %collective-permute-start.2 = (bf16[2,24,1024]{2,1,0:T(8,128)(2,1)}, bf16[2,24,1024]{2,1,0:T(8,128)(2,1)S(1)}, u32[]{:S(2)}, u32[]{:S(2)}) collective-permute-start(bf16[2,24,1024]{2,1,0:T(8,128)(2,1)} %get-tuple-element.25.refs_0_), channel_id=1, source_target_pairs={{0,3},{1,2},{2,1},{3,0},{4,7},{5,6},{6,5},{7,4},{8,11},{9,10},{10,... | collective-permute-start | bytes 294920 | tf_op jit(solution)/shard_map/ppermute | solution.py:403
  6.5 5.1 %collective-permute-start.1 = (bf16[2,24,1024]{2,1,0:T(8,128)(2,1)}, bf16[2,24,1024]{2,1,0:T(8,128)(2,1)S(1)}, u32[]{:S(2)}, u32[]{:S(2)}) collective-permute-start(bf16[2,24,1024]{2,1,0:T(8,128)(2,1)} %get-tuple-element.25.refs_0_), channel_id=1, source_target_pairs={{0,2},{1,3},{2,0},{3,1},{4,6},{5,7},{6,4},{7,5},{8,10},{9,11},{10,... | collective-permute-start | bytes 294920 | tf_op jit(solution)/shard_map/ppermute | solution.py:403
  7.0 4.9 %collective-permute-start = (bf16[2,24,1024]{2,1,0:T(8,128)(2,1)}, bf16[2,24,1024]{2,1,0:T(8,128)(2,1)S(1)}, u32[]{:S(2)}, u32[]{:S(2)}) collective-permute-start(bf16[2,24,1024]{2,1,0:T(8,128)(2,1)} %get-tuple-element.25.refs_0_), channel_id=1, source_target_pairs={{0,1},{1,0},{2,3},{3,2},{4,5},{5,4},{6,7},{7,6},{8,9},{9,8},{10,11... | collective-permute-start | bytes 294920 | tf_op jit(solution)/shard_map/ppermute | solution.py:403
  7.1 20.1 %collective-permute-start.15 = (bf16[24,6656]{1,0:T(8,128)(2,1)}, bf16[24,6656]{1,0:T(8,128)(2,1)S(1)}, u32[]{:S(2)}, u32[]{:S(2)}) collective-permute-start(bf16[24,6656]{1,0:T(8,128)(2,1)} %get-tuple-element.33.own), channel_id=1, source_target_pairs={{0,16},{4,20},{8,24},{12,28},{16,0},{20,4},{24,8},{28,12},{1,17},{... | collective-permute-start | bytes 958472 | tf_op jit(solution)/shard_map/ppermute | solution.py:195
  10.8 10.6 %copy-start.2 = (bf16[24,6656]{1,0:T(8,128)(2,1)S(1)}, bf16[24,6656]{1,0:T(8,128)(2,1)}, u32[]{:S(2)}) copy-start(bf16[24,6656]{1,0:T(8,128)(2,1)} %get-tuple-element.33.own) | copy-start | bytes 958468
  21.3 30.7 %collective-permute-start.3 = (bf16[4,24,3328]{2,1,0:T(8,128)(2,1)}, bf16[4,24,3328]{2,1,0:T(8,128)(2,1)S(1)}, u32[]{:S(2)}, u32[]{:S(2)}) collective-permute-start(bf16[4,24,3328]{2,1,0:T(8,128)(2,1)} %get-tuple-element.27), channel_id=1, source_target_pairs={{0,4},{4,0},{8,12},{12,8},{16,20},{20,16},{24,28},{28,24},{1,5},{5... | collective-permute-start | bytes 1916936 | tf_op jit(solution)/shard_map/ppermute | solution.py:199
  21.4 12.2 %collective-permute-start.14 = (bf16[24,6656]{1,0:T(8,128)(2,1)S(1)}, bf16[24,6656]{1,0:T(8,128)(2,1)S(1)}, u32[]{:S(2)}, u32[]{:S(2)}) collective-permute-start(bf16[24,6656]{1,0:T(8,128)(2,1)S(1)} %copy-done.2), channel_id=1, source_target_pairs={{8,0},{12,4},{16,8},{20,12},{24,16},{28,20},{9,1},{13,5},{17,9},{2... | collective-permute-start | bytes 958472 | tf_op jit(solution)/shard_map/ppermute | solution.py:195
  22.7 11.8 %collective-permute-start.13 = (bf16[24,6656]{1,0:T(8,128)(2,1)S(1)}, bf16[24,6656]{1,0:T(8,128)(2,1)S(1)}, u32[]{:S(2)}, u32[]{:S(2)}) collective-permute-start(bf16[24,6656]{1,0:T(8,128)(2,1)S(1)} %copy-done.2), channel_id=1, source_target_pairs={{0,8},{4,12},{8,16},{12,20},{16,24},{20,28},{1,9},{5,13},{9,17},{1... | collective-permute-start | bytes 958472 | tf_op jit(solution)/shard_map/ppermute | solution.py:195
  27.3 12.9 %copy-start.3 = (bf16[24,6656]{1,0:T(8,128)(2,1)}, bf16[24,6656]{1,0:T(8,128)(2,1)S(1)}, u32[]{:S(2)}) copy-start(bf16[24,6656]{1,0:T(8,128)(2,1)S(1)} %collective-permute-done.15.refs_2_) | copy-start | bytes 958468
  27.3 12.9 %collective-permute-start.16 = (bf16[24,6656]{1,0:T(8,128)(2,1)S(1)}, bf16[24,6656]{1,0:T(8,128)(2,1)S(1)}, u32[]{:S(2)}, u32[]{:S(2)}) collective-permute-start(bf16[24,6656]{1,0:T(8,128)(2,1)S(1)} %collective-permute-done.15.refs_2_), channel_id=1, source_target_pairs={{16,24},{20,28},{8,0},{12,4},{17,25},{21,29},{9,1},{13,5},{18,26},... | collective-permute-start | bytes 958472 | tf_op jit(solution)/shard_map/ppermute | solution.py:195
  43.5 58.5 %collective-permute-start.17 = (bf16[4,24,6656]{2,1,0:T(8,128)(2,1)}, bf16[4,24,6656]{2,1,0:T(8,128)(2,1)S(1)}, u32[]{:S(2)}, u32[]{:S(2)}) collective-permute-start(bf16[4,24,6656]{2,1,0:T(8,128)(2,1)} %shard_map.163.mine), channel_id=1, source_target_pairs={{0,4},{4,0},{8,12},{12,8},{16,20},{20,16},{24,28},{28,24},{1,5},{5... | collective-permute-start | bytes 3833864 | tf_op jit(solution)/shard_map/ppermute | solution.py:199
  55.3 6.2 %collective-permute-start.6 = (bf16[24,3328]{1,0:T(8,128)(2,1)}, bf16[24,3328]{1,0:T(8,128)(2,1)S(1)}, u32[]{:S(2)}, u32[]{:S(2)}) collective-permute-start(bf16[24,3328]{1,0:T(8,128)(2,1)} %get-tuple-element.32), channel_id=1, source_target_pairs={{24,16},{28,20},{0,8},{4,12},{25,17},{29,21},{1,9},{5,13},{26,18},... | collective-permute-start | bytes 479240 | tf_op jit(solution)/shard_map/ppermute | solution.py:195
  56.8 13.6 %collective-permute-start.4 = (bf16[24,3328]{1,0:T(8,128)(2,1)}, bf16[24,3328]{1,0:T(8,128)(2,1)S(1)}, u32[]{:S(2)}, u32[]{:S(2)}) collective-permute-start(bf16[24,3328]{1,0:T(8,128)(2,1)} %get-tuple-element.29), channel_id=1, source_target_pairs={{0,8},{4,12},{8,16},{12,20},{16,24},{20,28},{1,9},{5,13},{9,17},{1... | collective-permute-start | bytes 479240 | tf_op jit(solution)/shard_map/ppermute | solution.py:195
  58.1 12.3 %collective-permute-start.5 = (bf16[24,3328]{1,0:T(8,128)(2,1)}, bf16[24,3328]{1,0:T(8,128)(2,1)S(1)}, u32[]{:S(2)}, u32[]{:S(2)}) collective-permute-start(bf16[24,3328]{1,0:T(8,128)(2,1)} %get-tuple-element.30), channel_id=1, source_target_pairs={{8,0},{12,4},{16,8},{20,12},{24,16},{28,20},{9,1},{13,5},{17,9},{2... | collective-permute-start | bytes 479240 | tf_op jit(solution)/shard_map/ppermute | solution.py:195
  63.9 14.5 %collective-permute-start.7 = (bf16[24,3328]{1,0:T(8,128)(2,1)}, bf16[24,3328]{1,0:T(8,128)(2,1)S(1)}, u32[]{:S(2)}, u32[]{:S(2)}) collective-permute-start(bf16[24,3328]{1,0:T(8,128)(2,1)} %shard_map.160), channel_id=1, source_target_pairs={{0,16},{4,20},{8,24},{12,28},{16,0},{20,4},{24,8},{28,12},{1,17},{... | collective-permute-start | bytes 479240 | tf_op jit(solution)/shard_map/ppermute | solution.py:195
  70.4 8.1 %copy-start.8 = (bf16[24,3328]{1,0:T(8,128)(2,1)}, bf16[24,3328]{1,0:T(8,128)(2,1)S(1)}, u32[]{:S(2)}) copy-start(bf16[24,3328]{1,0:T(8,128)(2,1)S(1)} %collective-permute-done.4.refs_1_) | copy-start | bytes 479236
  81.0 10.4 %collective-permute-start.10 = (bf16[24,3328]{1,0:T(8,128)(2,1)}, bf16[24,3328]{1,0:T(8,128)(2,1)S(1)}, u32[]{:S(2)}, u32[]{:S(2)}) collective-permute-start(bf16[24,3328]{1,0:T(8,128)(2,1)} %shard_map.161.own), channel_id=1, source_target_pairs={{0,16},{4,20},{8,24},{12,28},{16,0},{20,4},{24,8},{28,12},{1,17},{... | collective-permute-start | bytes 479240 | tf_op jit(solution)/shard_map/ppermute | solution.py:195
  81.0 12.3 %collective-permute-start.9 = (bf16[24,3328]{1,0:T(8,128)(2,1)}, bf16[24,3328]{1,0:T(8,128)(2,1)S(1)}, u32[]{:S(2)}, u32[]{:S(2)}) collective-permute-start(bf16[24,3328]{1,0:T(8,128)(2,1)} %shard_map.161.own), channel_id=1, source_target_pairs={{8,0},{12,4},{16,8},{20,12},{24,16},{28,20},{9,1},{13,5},{17,9},{2... | collective-permute-start | bytes 479240 | tf_op jit(solution)/shard_map/ppermute | solution.py:195
  82.3 11.1 %collective-permute-start.8 = (bf16[24,3328]{1,0:T(8,128)(2,1)}, bf16[24,3328]{1,0:T(8,128)(2,1)S(1)}, u32[]{:S(2)}, u32[]{:S(2)}) collective-permute-start(bf16[24,3328]{1,0:T(8,128)(2,1)} %shard_map.161.own), channel_id=1, source_target_pairs={{0,8},{4,12},{8,16},{12,20},{16,24},{20,28},{1,9},{5,13},{9,17},{1... | collective-permute-start | bytes 479240 | tf_op jit(solution)/shard_map/ppermute | solution.py:195
  91.4 7.7 %collective-permute-start.11 = (bf16[24,3328]{1,0:T(8,128)(2,1)S(1)}, bf16[24,3328]{1,0:T(8,128)(2,1)S(1)}, u32[]{:S(2)}, u32[]{:S(2)}) collective-permute-start(bf16[24,3328]{1,0:T(8,128)(2,1)S(1)} %collective-permute-done.10.refs_2_), channel_id=1, source_target_pairs={{16,24},{20,28},{8,0},{12,4},{17,25},{21,29},{9,1},{13,5},{18,26},... | collective-permute-start | bytes 479240 | tf_op jit(solution)/shard_map/ppermute | solution.py:195
  101.9 14.2 %collective-permute-start.12 = (bf16[4,24,3328]{2,1,0:T(8,128)(2,1)}, bf16[4,24,3328]{2,1,0:T(8,128)(2,1)S(1)}, u32[]{:S(2)}, u32[]{:S(2)}) collective-permute-start(bf16[4,24,3328]{2,1,0:T(8,128)(2,1)} %shard_map.162.mine), channel_id=1, source_target_pairs={{0,4},{4,0},{8,12},{12,8},{16,20},{20,16},{24,28},{28,24},{1,5},{5... | collective-permute-start | bytes 1916936 | tf_op jit(solution)/shard_map/ppermute | solution.py:199
  136.8 17.9 %collective-permute-start.18 = (bf16[24,1024]{1,0:T(8,128)(2,1)}, bf16[24,1024]{1,0:T(8,128)(2,1)S(1)}, u32[]{:S(2)}, u32[]{:S(2)}) collective-permute-start(bf16[24,1024]{1,0:T(8,128)(2,1)} %get-tuple-element.37), channel_id=1, source_target_pairs={{0,1},{1,0},{2,3},{3,2},{4,5},{5,4},{6,7},{7,6},{8,9},{9,8},{10,11... | collective-permute-start | bytes 147464 | tf_op jit(solution)/shard_map/ppermute | solution.py:403
  138.3 16.4 %collective-permute-start.19 = (bf16[24,1024]{1,0:T(8,128)(2,1)}, bf16[24,1024]{1,0:T(8,128)(2,1)S(1)}, u32[]{:S(2)}, u32[]{:S(2)}) collective-permute-start(bf16[24,1024]{1,0:T(8,128)(2,1)} %get-tuple-element.38), channel_id=1, source_target_pairs={{0,2},{1,3},{2,0},{3,1},{4,6},{5,7},{6,4},{7,5},{8,10},{9,11},{10,... | collective-permute-start | bytes 147464 | tf_op jit(solution)/shard_map/ppermute | solution.py:403
  139.1 15.6 %collective-permute-start.20 = (bf16[24,1024]{1,0:T(8,128)(2,1)}, bf16[24,1024]{1,0:T(8,128)(2,1)S(1)}, u32[]{:S(2)}, u32[]{:S(2)}) collective-permute-start(bf16[24,1024]{1,0:T(8,128)(2,1)} %get-tuple-element.39), channel_id=1, source_target_pairs={{0,3},{1,2},{2,1},{3,0},{4,7},{5,6},{6,5},{7,4},{8,11},{9,10},{10,... | collective-permute-start | bytes 147464 | tf_op jit(solution)/shard_map/ppermute | solution.py:403
  (19 other events, 49.5 us)

commit v2 on v1

v2 whole, which is shorter than its diff:
```python
import functools

import jax
import jax.numpy as jnp
from jax import lax
from jax.experimental import pallas as pl
from jax.experimental.pallas import tpu as pltpu
from jax.sharding import Mesh
from jax.sharding import PartitionSpec as P

BLK_C = 128
F32 = jnp.float32
BF16 = jnp.bfloat16
VMEM = pltpu.VMEM
SMEM = pltpu.SMEM


def whole(space=VMEM):
    return pl.BlockSpec(memory_space=space)


def shape(dims, dtype):
    return jax.ShapeDtypeStruct(dims, dtype)


def params(mib=56):
    return pltpu.CompilerParams(vmem_limit_bytes=mib * 1024 * 1024)


def cost(flops, nbytes):
    return pl.CostEstimate(flops=int(flops), bytes_accessed=int(nbytes), transcendentals=0)


def pieces(extent, step):
    return [(at, min(step, extent - at)) for at in range(0, extent, step)]


def prep_kernel(xq, xs, xo, xc, gq, gs, go, gc, gate, up, xg, gu):
    for at, (quant, scale, flag, corr) in enumerate(((gq, gs, go, gc), (xq, xs, xo, xc))):
        for b in range(scale.shape[1]):
            cols = slice(b * BLK_C, (b + 1) * BLK_C)
            value = scale[0, b] * quant[:, cols].astype(F32) + flag[0, b].astype(F32) * corr[
                :, cols
            ].astype(F32)
            xg[at, :, cols] = value.astype(BF16)
    gu[...] = jnp.concatenate([gate[...].astype(F32), up[...].astype(F32)], 0).astype(BF16)


def prep(xq, xs, xo, xc, gq, gs, go, gc, gate, up):
    rows, width = xq.shape
    tok, ff = gate.shape
    return pl.pallas_call(
        prep_kernel,
        out_shape=(shape((2, rows, width), BF16), shape((2 * tok, ff), BF16)),
        in_specs=[whole(), whole(SMEM), whole(SMEM), whole()] * 2 + [whole()] * 2,
        out_specs=(whole(), whole()),
        compiler_params=params(),
        cost_estimate=cost(0, 4 * xq.size * 2 + gate.size * 8),
    )(xq, xs, xo, xc, gq, gs, go, gc, gate, up)


def load_down(start, width, w_hbm, w_vmem, sems):
    copies = []
    for k, (at, size) in enumerate(pieces(width, 256)):
        first = pl.multiple_of(start + at, 16)
        copy = pltpu.make_async_copy(
            w_hbm.at[pl.ds(first, size)], w_vmem.at[pl.ds(at, size)], sems.at[k]
        )
        copy.start()
        copies.append(copy)
    return copies


def hidden_half(copies, grads_t, width, w_vmem, out):
    groups, rows = out.shape[0], out.shape[1]
    for copy, (at, size) in zip(copies, pieces(width, 256)):
        copy.wait()
        total = jnp.dot(w_vmem[at : at + size, :], grads_t, preferred_element_type=F32).T
        for q in range(groups):
            out[q, :, at : at + size] = total[q * rows : (q + 1) * rows, :].astype(out.dtype)


def first_half_kernel(n_t, offset, place, *refs):
    parts, (w_hbm, grads_out, grads_t, inputs_t, out, w_vmem, held, sems) = refs[:n_t], refs[n_t:]
    core, me = place[0], place[2]
    width = out.shape[2]
    copies = load_down((1 - core) * offset, width, w_hbm, w_vmem, sems)
    rows = held.shape[1]
    for s in range(n_t):
        held[me ^ s] = parts[s][1].astype(F32)
    inputs_t[...] = held[...].reshape(n_t * rows, held.shape[2]).T.astype(BF16)
    for s in range(n_t):
        held[me ^ s] = parts[s][0].astype(F32)
    grads = held[...].reshape(n_t * rows, held.shape[2])
    grads_out[...] = grads.astype(BF16)
    grads_t[...] = grads.T.astype(BF16)
    hidden_half(copies, grads_t[...], width, w_vmem, out)


def second_half_kernel(offset, place, grads_t, w_hbm, out, w_vmem, sems):
    width = out.shape[2]
    copies = load_down(place[0] * offset, width, w_hbm, w_vmem, sems)
    hidden_half(copies, grads_t[...], width, w_vmem, out)


def first_half(place, parts, w_down, n_z, width):
    n_t, rows, chans = len(parts), parts[0].shape[1], parts[0].shape[2]
    tokens = n_t * rows
    n_copies = len(pieces(width, 256))
    return pl.pallas_call(
        functools.partial(first_half_kernel, n_t, w_down.shape[0] - width),
        out_shape=(
            shape((tokens, chans), BF16),
            shape((chans, tokens), BF16),
            shape((chans, tokens), BF16),
            shape((n_z, tokens // n_z, width), BF16),
        ),
        in_specs=[whole(SMEM)] + [whole()] * n_t + [whole(pl.ANY)],
        out_specs=(whole(),) * 4,
        scratch_shapes=[
            VMEM((width, chans), BF16),
            VMEM((n_t, rows, chans), F32),
            pltpu.SemaphoreType.DMA((n_copies,)),
        ],
        compiler_params=params(),
        cost_estimate=cost(2 * tokens * chans * width, 2 * chans * width),
    )(place, *parts, w_down)


def second_half(place, grads_t, w_down, n_z, width):
    chans, tokens = grads_t.shape
    n_copies = len(pieces(width, 256))
    return pl.pallas_call(
        functools.partial(second_half_kernel, w_down.shape[0] - width),
        out_shape=shape((n_z, tokens // n_z, width), F32),
        in_specs=[whole(SMEM), whole(), whole(pl.ANY)],
        out_specs=whole(),
        scratch_shapes=[VMEM((width, chans), BF16), pltpu.SemaphoreType.DMA((n_copies,))],
        compiler_params=params(),
        cost_estimate=cost(2 * tokens * chans * width, 2 * chans * width),
    )(place, grads_t, w_down)


def pair_kernel(mine, theirs, out):
    out[...] = (mine[...] + theirs[...].astype(F32)).astype(BF16)


def pair_sum(mine, theirs):
    return pl.pallas_call(
        pair_kernel,
        out_shape=shape(mine.shape, BF16),
        in_specs=[whole(), whole()],
        out_specs=whole(),
        compiler_params=params(),
        cost_estimate=cost(0, mine.size * 8),
    )(mine, theirs)


def spread_kernel(parts, out):
    total = parts[0].astype(F32)
    for q in range(1, parts.shape[0]):
        total = total + parts[q].astype(F32)
    for q in range(parts.shape[0]):
        out[q] = total.astype(BF16)


def spread_sum(parts):
    return pl.pallas_call(
        spread_kernel,
        out_shape=shape(parts.shape, BF16),
        in_specs=[whole()],
        out_specs=whole(),
        compiler_params=params(),
        cost_estimate=cost(0, parts.size * 4),
    )(parts)


def add_kernel(*refs):
    *terms, out = refs
    total = terms[0][...].astype(F32)
    for term in terms[1:]:
        total = total + term[...].astype(F32)
    out[...] = total.astype(out.dtype)


def add_all(*terms):
    return pl.pallas_call(
        add_kernel,
        out_shape=shape(terms[0].shape, BF16),
        in_specs=[whole()] * len(terms),
        out_specs=whole(),
        compiler_params=params(),
        cost_estimate=cost(0, terms[0].size * 2 * (len(terms) + 2)),
    )(*terms)


def down_kernel(place, mine, theirs, grads, out_hbm, gate_factor, up_factor, out, sems):
    core0 = place[0] == 0
    n_z, double, ff = mine.shape
    tok = double // 2
    copies = []
    for k, (at, size) in enumerate(pieces(ff, 512)):
        cols = slice(at, at + size)
        gate, up = [], []
        for q in range(n_z):
            a, b = mine[q, :, cols].astype(F32), theirs[q, :, cols].astype(F32)
            first, second = jnp.where(core0, a, b), jnp.where(core0, b, a)
            gate += [first[:tok], second[:tok]]
            up += [first[tok:], second[tok:]]
        gate, up = jnp.concatenate(gate, 0), jnp.concatenate(up, 0)
        sig = 1.0 / (1.0 + jnp.exp(-gate))
        silu = gate * sig
        hidden = silu * up
        gate_factor[:, cols] = up * sig * (1.0 + gate * (1.0 - sig))
        up_factor[:, cols] = silu
        out[cols, :] = jnp.dot(
            hidden.T.astype(BF16), grads[...], preferred_element_type=F32
        ).astype(BF16)
        copy = pltpu.make_async_copy(out.at[cols], out_hbm.at[cols], sems.at[k])
        copy.start()
        copies.append(copy)
    for copy in copies:
        copy.wait()


def down_grad(place, mine, theirs, grads):
    n_z, double, ff = mine.shape
    tokens, chans = grads.shape
    return pl.pallas_call(
        down_kernel,
        out_shape=(shape((ff, chans), BF16), shape((tokens, ff), F32), shape((tokens, ff), F32)),
        in_specs=[whole(SMEM)] + [whole()] * 3,
        out_specs=(whole(pl.ANY), whole(), whole()),
        scratch_shapes=[
            VMEM((ff, chans), BF16), pltpu.SemaphoreType.DMA((len(pieces(ff, 512)),))
        ],
        compiler_params=params(),
        cost_estimate=cost(2 * tokens * chans * ff, 2 * chans * ff + 8 * tokens * ff),
    )(place, mine, theirs, grads)


def input_kernel(n_t, place, mine, theirs, gate_factor, up_factor, gate_hbm, up_hbm, *refs):
    (gate_grad, up_grad), pieces_out = refs[:2], refs[2 : 2 + n_t]
    w_gate, w_up, total, held, sems = refs[2 + n_t :]
    core0 = place[0] == 0
    n_z, rows, width = mine.shape
    ff = gate_grad.shape[1]
    low = ff - width
    parts = [(0, at, size) for at, size in pieces(low, 512)]
    parts += [(low, at, size) for at, size in pieces(width, 512)]
    copies = []
    for k, (base, at, size) in enumerate(parts):
        cols = slice(base + at, base + at + size)
        pair = [
            pltpu.make_async_copy(hbm.at[:, cols], vmem.at[:, cols], sems.at[n, k])
            for n, (hbm, vmem) in enumerate(((gate_hbm, w_gate), (up_hbm, w_up)))
        ]
        for copy in pair:
            copy.start()
        copies.append(pair)
    dims = (((1,), (1,)), ((), ()))
    for k, (base, at, size) in enumerate(parts):
        cols = slice(base + at, base + at + size)
        first = core0 if base == 0 else ~core0
        hidden = jnp.concatenate(
            [
                jnp.where(first, mine[q, :, at : at + size], theirs[q, :, at : at + size]).astype(F32)
                for q in range(n_z)
            ],
            0,
        )
        gate = (hidden * gate_factor[:, cols]).astype(BF16)
        up = (hidden * up_factor[:, cols]).astype(BF16)
        gate_grad[:, cols] = gate
        up_grad[:, cols] = up
        for copy in copies[k]:
            copy.wait()
        term = lax.dot_general(w_gate[:, cols], gate, dims, preferred_element_type=F32)
        term += lax.dot_general(w_up[:, cols], up, dims, preferred_element_type=F32)
        total[...] = term if k == 0 else total[...] + term
    held[...] = total[...].T.reshape(held.shape)
    for s, out in enumerate(pieces_out):
        out[...] = held[place[2] ^ s].astype(out.dtype)


def input_grad(place, mine, theirs, gate_factor, up_factor, w_gate, w_up, n_t):
    tokens, ff = gate_factor.shape
    chans = w_gate.shape[0]
    rows, width = tokens // n_t, mine.shape[2]
    n_copies = len(pieces(ff - width, 512)) + len(pieces(width, 512))
    return pl.pallas_call(
        functools.partial(input_kernel, n_t),
        out_shape=(shape((tokens, ff), BF16),) * 2
        + (shape((rows, chans), F32),)
        + (shape((rows, chans), BF16),) * (n_t - 1),
        in_specs=[whole(SMEM)] + [whole()] * 4 + [whole(pl.ANY)] * 2,
        out_specs=(whole(),) * (2 + n_t),
        scratch_shapes=[
            VMEM((chans, ff), BF16),
            VMEM((chans, ff), BF16),
            VMEM((chans, tokens), F32),
            VMEM((n_t, rows, chans), F32),
            pltpu.SemaphoreType.DMA((2, n_copies)),
        ],
        compiler_params=params(),
        cost_estimate=cost(4 * tokens * chans * ff, 4 * chans * ff + 12 * tokens * ff),
    )(place, mine, theirs, gate_factor, up_factor, w_gate, w_up)


def weight_kernel(inputs_t, gate_grad, up_grad, gate_hbm, up_hbm, gate_out, up_out, sems):
    copies = []
    ff = gate_grad.shape[1]
    for n, (grad, out, hbm) in enumerate(
        ((gate_grad, gate_out, gate_hbm), (up_grad, up_out, up_hbm))
    ):
        for k, (at, size) in enumerate(pieces(ff, 512)):
            cols = slice(at, at + size)
            out[:, cols] = jnp.dot(
                inputs_t[...], grad[:, cols], preferred_element_type=F32
            ).astype(BF16)
            copy = pltpu.make_async_copy(out.at[:, cols], hbm.at[:, cols], sems.at[n, k])
            copy.start()
            copies.append(copy)
    for copy in copies:
        copy.wait()


def weight_grads(inputs_t, gate_grad, up_grad):
    chans, tokens = inputs_t.shape
    ff = gate_grad.shape[1]
    return pl.pallas_call(
        weight_kernel,
        out_shape=(shape((chans, ff), BF16),) * 2,
        in_specs=[whole()] * 3,
        out_specs=(whole(pl.ANY),) * 2,
        scratch_shapes=[VMEM((chans, ff), BF16)] * 2
        + [pltpu.SemaphoreType.DMA((2, len(pieces(ff, 512))))],
        compiler_params=params(),
        cost_estimate=cost(4 * tokens * chans * ff, 4 * chans * ff + 4 * tokens * ff),
    )(inputs_t, gate_grad, up_grad)


def on_device(n_z, n_t, xq, xs, xo, xc, gq, gs, go, gc, gate_pre, up_pre, w_gate, w_up, w_down):
    place = jnp.stack([lax.axis_index(name) for name in ("core", "z", "tensor")]).astype(jnp.int32)
    ff = gate_pre.shape[1]
    width = -(-ff // 256) * 128

    def to_tensor(value, s):
        return lax.ppermute(value, "tensor", [(a, a ^ s) for a in range(n_t)])

    def to_core(value):
        return lax.ppermute(value, "core", [(0, 1), (1, 0)])

    def to_chips(value):
        return lax.all_to_all(value, "z", 0, 0, tiled=True)

    own, gate_up = prep(xq, xs, xo, xc, gq, gs, go, gc, gate_pre, up_pre)
    parts = [own] + [to_tensor(own, s) for s in range(1, n_t)]
    gate_up = lax.all_gather(gate_up, "z")
    grads, grads_t, inputs_t, send = first_half(place, parts, w_down, n_z, width)
    got = to_core(send)
    mine = second_half(place, grads_t, w_down, n_z, width)
    hidden_grad = to_chips(spread_sum(to_chips(pair_sum(mine, got))))
    grad_down, gate_factor, up_factor = down_grad(place, gate_up, to_core(gate_up), grads)
    gate_grad, up_grad, kept, *sends = input_grad(
        place, hidden_grad, to_core(hidden_grad), gate_factor, up_factor, w_gate, w_up, n_t
    )
    terms = [to_tensor(part, s) for s, part in enumerate(sends, 1)]
    grad_gate, grad_up = weight_grads(inputs_t, gate_grad, up_grad)
    return add_all(kept, *terms), grad_gate, grad_up, grad_down


def solution(mesh):
    n_dp, n_t = mesh.shape["dp"], mesh.shape["tensor"]
    fine = Mesh(mesh.devices.reshape(n_dp // 2, 2, n_t), ("z", "core", "tensor"))
    by_token, by_dp = P("tensor", ("z", "core")), P(("z", "core"), "tensor")
    return jax.shard_map(
        functools.partial(on_device, n_dp // 2, n_t),
        mesh=fine,
        in_specs=(by_token,) * 8 + (by_dp,) * 4 + (by_token,),
        out_specs=(by_token, by_dp, by_dp, by_token),
        check_vma=False,
    )
```

time: 159 us -> 136 us (0.86); the launches traced: 157 us -> 136 us
  starting transfers between devices: 37.2 us -> 11.9 us
  blocking collectives: 0 us -> 23.3 us
  Pallas kernels: 78.5 us -> 60.8 us
  between operations: 0.9 us -> 14.2 us
  waiting for transfers between devices: 32.7 us -> 20.8 us
  local copies, waits for them, and re-layouts: 6.99 us -> 4.27 us
    ppermute x15 -> x3, waiting for transfers between devices: 31.5 us -> 0.01 us  [to_core(): return lax.ppermute(value, 'core', [(0, 1), (1, 0)])]
    ppermute x15 -> x3, starting transfers between devices: 29.2 us -> 0.14 us  [to_core(): return lax.ppermute(value, 'core', [(0, 1), (1, 0)])]
    all_to_all x0 -> x1, blocking collectives: none -> 23.3 us  [to_chips(): return lax.all_to_all(value, 'z', 0, 0, tiled=True)]
    all_to_all x0 -> x1, waiting for transfers between devices: none -> 16.5 us  [to_chips(): return lax.all_to_all(value, 'z', 0, 0, tiled=True)]
    pallas_call x6 -> x5, Pallas kernels: 54.5 us -> 42.1 us  [the longest x1 16.8 us: input_grad(): pl.pallas_call(functools.partial(input_kernel, n_t), out_shape=(shape((to...]
    all_to_all x0 -> x1, starting transfers between devices: none -> 3.66 us  [to_chips(): return lax.all_to_all(value, 'z', 0, 0, tiled=True)]
    pallas_call x3 -> x1, Pallas kernels: 5.16 us -> 1.57 us  [add_all(): pl.pallas_call(add_kernel, out_shape=shape(terms[0].shape, BF16), in_spec...]
    ppermute x6, waiting for transfers between devices: 1.2 us -> 4.24 us  [to_tensor(): return lax.ppermute(value, 'tensor', [(a, a ^ s) for a in range(n_t)])]
  transfers between devices with their start and end apart: 21 -> 11, of which waited for: 10 -> 4; matrix products, arithmetic and copies ran while one was open for 0% -> 0% of each run, Pallas kernels for 35% -> 30%
where the time goes in v2:
time: 136 us
  Pallas kernels  60.8 us (45%)
  blocking collectives  23.3 us (17%)
  waiting for transfers between devices  20.8 us (15%)
  between operations  14.2 us (10%)
  starting transfers between devices  11.9 us (9%)
  local copies, waits for them, and re-layouts  4.27 us (3%)
    all_to_all x1, blocking collectives, to_chips(): return lax.all_to_all(value, 'z', 0, 0, tiled=True)  23.3 us
    pallas_call x1, Pallas kernels, input_grad(): pl.pallas_call(functools.partial(input_kernel, n_t), out_shape=(shape((to...  16.8 us
    all_to_all x1, waiting for transfers between devices, to_chips(): return lax.all_to_all(value, 'z', 0, 0, tiled=True)  16.5 us
    pallas_call x1, Pallas kernels, weight_grads(): pl.pallas_call(weight_kernel, out_shape=(shape((chans, ff), BF16),) * 2,...  11.4 us
    pallas_call x1, Pallas kernels, down_grad(): pl.pallas_call(down_kernel, out_shape=(shape((ff, chans), BF16), shape((t...  9.51 us
    ppermute x6, starting transfers between devices, to_tensor(): return lax.ppermute(value, 'tensor', [(a, a ^ s) for a in range(n_t)])  8.04 us
    pallas_call x1, Pallas kernels, second_half(): pl.pallas_call(functools.partial(second_half_kernel, w_down.shape[0] - wi...  7.65 us
    pallas_call x1, Pallas kernels, first_half(): pl.pallas_call(functools.partial(first_half_kernel, n_t, w_down.shape[0]...  7.53 us
  transfers between devices with their start and end apart: 11, of which 4 were waited for; matrix products, arithmetic and copies ran while one was open for 0% of the time, Pallas kernels for 30%

profile of v2, /device:TPU:0, one launch (start us, length us, event | category | flops | bytes accessed | tf_op | source)
XLA Modules:
  0.0 135.9 jit_solution(13190993211873929191)
XLA Ops:
  7.2 2.0 %shard_map.156 = (bf16[2,24,1024]{2,1,0:T(8,128)(2,1)}, bf16[24,6656]{1,0:T(8,128)(2,1)}) custom-call(bf16[24,1024]{1,0:T(8,128)(2,1)} %xq.1, f32[1,8]{1,0:T(1,128)} %xs.1, s32[1,8]{1,0:T(1,128)} %xo.1, bf16[24,1024]{1,0:T(8,128)(2,1)} %xc.1, bf16[24,1024]{1,0:T(8,128)(2,1)} %gq.1, f32[1,8]{1,0:T(1,128)} %gs.1, s32[1,8]{1,0:T(1,128)} %go.1, ...), custom_call_target="tpu_custom_call" | custom-call | bytes 835584 | tf_op jit(solution)/shard_map/pallas_call | solution.py:52
  9.2 3.9 %collective-permute-start.2 = (bf16[2,24,1024]{2,1,0:T(8,128)(2,1)}, bf16[2,24,1024]{2,1,0:T(8,128)(2,1)S(1)}, u32[]{:S(2)}, u32[]{:S(2)}) collective-permute-start(bf16[2,24,1024]{2,1,0:T(8,128)(2,1)} %get-tuple-element.21.refs_0_), channel_id=1, source_target_pairs={{0,3},{1,2},{2,1},{3,0},{4,7},{5,6},{6,5},{7,4},{8,11},{9,10},{10,... | collective-permute-start | bytes 294920 | tf_op jit(solution)/shard_map/ppermute | solution.py:349
  13.1 0.5 collective-permute-start.1
  13.7 0.6 pad_add_fusion.place
  14.3 2.3 %collective-permute-done.2.refs_3_ = bf16[2,24,1024]{2,1,0:T(8,128)(2,1)S(1)} collective-permute-done((bf16[2,24,1024]{2,1,0:T(8,128)(2,1)}, bf16[2,24,1024]{2,1,0:T(8,128)(2,1)S(1)}, u32[]{:S(2)}, u32[]{:S(2)}) %collective-permute-start.2) | collective-permute-done | bytes 98336 | tf_op jit(solution)/shard_map/ppermute | solution.py:349
  16.6 1.6 %collective-permute-done.1.refs_2_ = bf16[2,24,1024]{2,1,0:T(8,128)(2,1)S(1)} collective-permute-done((bf16[2,24,1024]{2,1,0:T(8,128)(2,1)}, bf16[2,24,1024]{2,1,0:T(8,128)(2,1)S(1)}, u32[]{:S(2)}, u32[]{:S(2)}) %collective-permute-start.1) | collective-permute-done | bytes 98336 | tf_op jit(solution)/shard_map/ppermute | solution.py:349
  18.8 0.6 copy-done.5
  19.5 7.5 %shard_map.157 = (bf16[96,1024]{1,0:T(8,128)(2,1)}, bf16[1024,96]{1,0:T(8,128)(2,1)}, bf16[1024,96]{1,0:T(8,128)(2,1)}, bf16[4,24,3328]{2,1,0:T(8,128)(2,1)}) custom-call(s32[3]{0:T(128)} %pad_add_fusion.place, bf16[2,24,1024]{2,1,0:T(8,128)(2,1)} %get-tuple-element.21.refs_0_, bf16[2,24,1024]{2,1,0:T(8,128)(2,1)} %copy-done.5, ...), custom_call_target="tpu_custom_call" | custom-call | flops 654311424 | bytes 6815744 | tf_op jit(solution)/shard_map/pallas_call | solution.py:110
  27.1 7.7 %shard_map.158.mine = f32[4,24,3328]{2,1,0:T(8,128)} custom-call(s32[3]{0:T(128)} %pad_add_fusion.place, bf16[1024,96]{1,0:T(8,128)(2,1)} %get-tuple-element.22.grads_t, bf16[6656,1024]{1,0:T(8,128)(2,1)} %w_hbm.1), custom_call_target="tpu_custom_call" | custom-call | flops 654311424 | bytes 6815744 | tf_op jit(solution)/shard_map/pallas_call | solution.py:133
  34.8 0.8 copy-done.1
  35.6 2.4 %shard_map.159 = bf16[4,24,3328]{2,1,0:T(8,128)(2,1)} custom-call(f32[4,24,3328]{2,1,0:T(8,128)} %shard_map.158.mine, bf16[4,24,3328]{2,1,0:T(8,128)(2,1)} %copy-done.1), custom_call_target="tpu_custom_call" | custom-call | bytes 2555904 | tf_op jit(solution)/shard_map/pallas_call | solution.py:149
  38.0 23.3 %all_to_all.10.parts = bf16[4,24,3328]{2,1,0:T(8,128)(2,1)} all-to-all(bf16[4,24,3328]{2,1,0:T(8,128)(2,1)} %shard_map.159), channel_id=1, replica_groups=mesh['z'=4,'core'=2,'tensor'=4] {'z'}, dimensions={0} | all-to-all | bytes 1277952 | tf_op jit(solution)/shard_map/all_to_all | solution.py:355
  61.2 2.0 %shard_map.160 = bf16[4,24,3328]{2,1,0:T(8,128)(2,1)} custom-call(bf16[4,24,3328]{2,1,0:T(8,128)(2,1)} %all_to_all.10.parts), custom_call_target="tpu_custom_call" | custom-call | bytes 1277952 | tf_op jit(solution)/shard_map/pallas_call | solution.py:168
  63.2 3.7 %all-to-all-start.1 = ((bf16[4,24,3328]{2,1,0:T(8,128)(2,1)}), bf16[4,24,3328]{2,1,0:T(8,128)(2,1)S(1)}, u32[]{:S(2)}, u32[]{:S(2)}) async-start(bf16[4,24,3328]{2,1,0:T(8,128)(2,1)} %shard_map.160), calls=%async_computation.1 | async-start | bytes 1277952 | tf_op jit(solution)/shard_map/all_to_all | solution.py:355
  67.0 16.5 %all-to-all-done.1.mine = bf16[4,24,3328]{2,1,0:T(8,128)(2,1)S(1)} async-done(((bf16[4,24,3328]{2,1,0:T(8,128)(2,1)}), bf16[4,24,3328]{2,1,0:T(8,128)(2,1)S(1)}, u32[]{:S(2)}, u32[]{:S(2)}) %all-to-all-start.1) | async-done | bytes 639008 | tf_op jit(solution)/shard_map/all_to_all | solution.py:355
  83.6 1.1 copy-done.9
  84.6 9.5 %shard_map.161 = (bf16[6656,1024]{1,0:T(8,128)(2,1)}, f32[96,6656]{1,0:T(8,128)}, f32[96,6656]{1,0:T(8,128)}) custom-call(s32[3]{0:T(128)} %pad_add_fusion.place, bf16[4,24,6656]{2,1,0:T(8,128)(2,1)} %bitcast.5, bf16[4,24,6656]{2,1,0:T(8,128)(2,1)} %copy-done.9, bf16[96,1024]{1,0:T(8,128)(2,1)} %get-tuple-element.25.grads), custom_call_target="tpu_custom_call" | custom-call | flops 1308622848 | bytes 18743296 | tf_op jit(solution)/shard_map/pallas_call | solution.py:229
  94.2 0.8 copy-done.2
  95.0 16.8 %shard_map.162 = (bf16[96,6656]{1,0:T(8,128)(2,1)}, bf16[96,6656]{1,0:T(8,128)(2,1)}, f32[24,1024]{1,0:T(8,128)}, bf16[24,1024]{1,0:T(8,128)(2,1)}, bf16[24,1024]{1,0:T(8,128)(2,1)}, /*index=5*/bf16[24,1024]{1,0:T(8,128)(2,1)}) custom-call(s32[3]{0:T(128)} %pad_add_fusion.place, bf16[4,24,3328]{2,1,0:T(8,128)(2,1)} %copy-done, ...), custom_call_target="tpu_custom_call" | custom-call | flops 2617245696 | bytes 34930688 | tf_op jit(solution)/shard_map/pallas_call | solution.py:291
  111.8 1.6 %collective-permute-start.6 = (bf16[24,1024]{1,0:T(8,128)(2,1)}, bf16[24,1024]{1,0:T(8,128)(2,1)S(1)}, u32[]{:S(2)}, u32[]{:S(2)}) collective-permute-start(bf16[24,1024]{1,0:T(8,128)(2,1)} %get-tuple-element.29), channel_id=1, source_target_pairs={{0,1},{1,0},{2,3},{3,2},{4,5},{5,4},{6,7},{7,6},{8,9},{9,8},{10,11... | collective-permute-start | bytes 147464 | tf_op jit(solution)/shard_map/ppermute | solution.py:349
  113.4 1.9 %collective-permute-start.7 = (bf16[24,1024]{1,0:T(8,128)(2,1)}, bf16[24,1024]{1,0:T(8,128)(2,1)S(1)}, u32[]{:S(2)}, u32[]{:S(2)}) collective-permute-start(bf16[24,1024]{1,0:T(8,128)(2,1)} %get-tuple-element.30), channel_id=1, source_target_pairs={{0,2},{1,3},{2,0},{3,1},{4,6},{5,7},{6,4},{7,5},{8,10},{9,11},{10,... | collective-permute-start | bytes 147464 | tf_op jit(solution)/shard_map/ppermute | solution.py:349
  115.4 11.4 %shard_map.164 = (bf16[1024,6656]{1,0:T(8,128)(2,1)}, bf16[1024,6656]{1,0:T(8,128)(2,1)}) custom-call(bf16[1024,96]{1,0:T(8,128)(2,1)} %get-tuple-element.32.inputs_t, bf16[96,6656]{1,0:T(8,128)(2,1)} %get-tuple-element.33.gate_grad, bf16[96,6656]{1,0:T(8,128)(2,1)} %get-tuple-element.34.up_grad), custom_call_target="tpu_custom_call" | custom-call | flops 2617245696 | bytes 29818880 | tf_op jit(solution)/shard_map/pallas_call | solution.py:331
  126.8 0.6 copy-done.6
  127.5 1.6 %shard_map.163 = bf16[24,1024]{1,0:T(8,128)(2,1)} custom-call(f32[24,1024]{1,0:T(8,128)} %get-tuple-element.28.refs_0_, bf16[24,1024]{1,0:T(8,128)(2,1)} %copy-done.6, bf16[24,1024]{1,0:T(8,128)(2,1)} %copy-done.7, bf16[24,1024]{1,0:T(8,128)(2,1)} %copy-done.8), custom_call_target="tpu_custom_call" | custom-call | bytes 294912 | tf_op jit(solution)/shard_map/pallas_call | solution.py:187
  (30 shorter events, 1.1 us)
Async XLA Ops:
  7.2 59.8 %all-gather.3.cloned.1.call-start = ((), (), s32[]{:S(2)}) async-start(), calls=%async_computation.2 | async-start | bytes 1597440 | tf_op jit(solution)/shard_map/all_gather | solution.py:359
  9.2 7.4 %collective-permute-start.2 = (bf16[2,24,1024]{2,1,0:T(8,128)(2,1)}, bf16[2,24,1024]{2,1,0:T(8,128)(2,1)S(1)}, u32[]{:S(2)}, u32[]{:S(2)}) collective-permute-start(bf16[2,24,1024]{2,1,0:T(8,128)(2,1)} %get-tuple-element.21.refs_0_), channel_id=1, source_target_pairs={{0,3},{1,2},{2,1},{3,0},{4,7},{5,6},{6,5},{7,4},{8,11},{9,10},{10,... | collective-permute-start | bytes 294920 | tf_op jit(solution)/shard_map/ppermute | solution.py:349
  13.1 5.1 %collective-permute-start.1 = (bf16[2,24,1024]{2,1,0:T(8,128)(2,1)}, bf16[2,24,1024]{2,1,0:T(8,128)(2,1)S(1)}, u32[]{:S(2)}, u32[]{:S(2)}) collective-permute-start(bf16[2,24,1024]{2,1,0:T(8,128)(2,1)} %get-tuple-element.21.refs_0_), channel_id=1, source_target_pairs={{0,2},{1,3},{2,0},{3,1},{4,6},{5,7},{6,4},{7,5},{8,10},{9,11},{10,... | collective-permute-start | bytes 294920 | tf_op jit(solution)/shard_map/ppermute | solution.py:349
  13.6 4.9 %collective-permute-start = (bf16[2,24,1024]{2,1,0:T(8,128)(2,1)}, bf16[2,24,1024]{2,1,0:T(8,128)(2,1)S(1)}, u32[]{:S(2)}, u32[]{:S(2)}) collective-permute-start(bf16[2,24,1024]{2,1,0:T(8,128)(2,1)} %get-tuple-element.21.refs_0_), channel_id=1, source_target_pairs={{0,1},{1,0},{2,3},{3,2},{4,5},{5,4},{6,7},{7,6},{8,9},{9,8},{10,11... | collective-permute-start | bytes 294920 | tf_op jit(solution)/shard_map/ppermute | solution.py:349
  16.6 2.0 %copy-start.3 = (bf16[2,24,1024]{2,1,0:T(8,128)(2,1)}, bf16[2,24,1024]{2,1,0:T(8,128)(2,1)S(1)}, u32[]{:S(2)}) copy-start(bf16[2,24,1024]{2,1,0:T(8,128)(2,1)S(1)} %collective-permute-done.2.refs_3_) | copy-start | bytes 294916
  18.2 0.6 copy-start.4
  18.8 0.6 copy-start.5
  27.0 7.7 %collective-permute-start.3 = (bf16[4,24,3328]{2,1,0:T(8,128)(2,1)}, bf16[4,24,3328]{2,1,0:T(8,128)(2,1)S(1)}, u32[]{:S(2)}, u32[]{:S(2)}) collective-permute-start(bf16[4,24,3328]{2,1,0:T(8,128)(2,1)} %get-tuple-element.23), channel_id=1, source_target_pairs={{0,4},{4,0},{1,5},{5,1},{2,6},{6,2},{3,7},{7,3},{8,12},{12,8},{9,1... | collective-permute-start | bytes 1916936 | tf_op jit(solution)/shard_map/ppermute | solution.py:352
  34.8 0.8 copy-start.1
  63.2 20.3 %all-to-all-start.1 = ((bf16[4,24,3328]{2,1,0:T(8,128)(2,1)}), bf16[4,24,3328]{2,1,0:T(8,128)(2,1)S(1)}, u32[]{:S(2)}, u32[]{:S(2)}) async-start(bf16[4,24,3328]{2,1,0:T(8,128)(2,1)} %shard_map.160), calls=%async_computation.1 | async-start | bytes 1277952 | tf_op jit(solution)/shard_map/all_to_all | solution.py:355
  66.9 16.6 %collective-permute-start.5 = (bf16[4,24,6656]{2,1,0:T(8,128)(2,1)}, bf16[4,24,6656]{2,1,0:T(8,128)(2,1)S(1)}, u32[]{:S(2)}, u32[]{:S(2)}) collective-permute-start(bf16[4,24,6656]{2,1,0:T(8,128)(2,1)} %bitcast.4), channel_id=1, source_target_pairs={{0,4},{4,0},{1,5},{5,1},{2,6},{6,2},{3,7},{7,3},{8,12},{12,8},{9,1... | collective-permute-start | bytes 3833864 | tf_op jit(solution)/shard_map/ppermute | solution.py:352
  83.6 10.6 %copy-start = (bf16[4,24,3328]{2,1,0:T(8,128)(2,1)}, bf16[4,24,3328]{2,1,0:T(8,128)(2,1)S(1)}, u32[]{:S(2)}) copy-start(bf16[4,24,3328]{2,1,0:T(8,128)(2,1)S(1)} %all-to-all-done.1.mine) | copy-start | bytes 1916932
  83.6 10.6 %collective-permute-start.4 = (bf16[4,24,3328]{2,1,0:T(8,128)(2,1)S(1)}, bf16[4,24,3328]{2,1,0:T(8,128)(2,1)S(1)}, u32[]{:S(2)}, u32[]{:S(2)}) collective-permute-start(bf16[4,24,3328]{2,1,0:T(8,128)(2,1)S(1)} %all-to-all-done.1.mine), channel_id=1, source_target_pairs={{0,4},{4,0},{1,5},{5,1},{2,6},{6,2},{3,7},{7,3},{8,12},{12,8},{9,1... | collective-permute-start | bytes 1916936 | tf_op jit(solution)/shard_map/ppermute | solution.py:352
  83.6 1.1 copy-start.9
  94.2 0.8 copy-start.2
  111.8 14.9 %collective-permute-start.6 = (bf16[24,1024]{1,0:T(8,128)(2,1)}, bf16[24,1024]{1,0:T(8,128)(2,1)S(1)}, u32[]{:S(2)}, u32[]{:S(2)}) collective-permute-start(bf16[24,1024]{1,0:T(8,128)(2,1)} %get-tuple-element.29), channel_id=1, source_target_pairs={{0,1},{1,0},{2,3},{3,2},{4,5},{5,4},{6,7},{7,6},{8,9},{9,8},{10,11... | collective-permute-start | bytes 147464 | tf_op jit(solution)/shard_map/ppermute | solution.py:349
  113.4 13.4 %collective-permute-start.7 = (bf16[24,1024]{1,0:T(8,128)(2,1)}, bf16[24,1024]{1,0:T(8,128)(2,1)S(1)}, u32[]{:S(2)}, u32[]{:S(2)}) collective-permute-start(bf16[24,1024]{1,0:T(8,128)(2,1)} %get-tuple-element.30), channel_id=1, source_target_pairs={{0,2},{1,3},{2,0},{3,1},{4,6},{5,7},{6,4},{7,5},{8,10},{9,11},{10,... | collective-permute-start | bytes 147464 | tf_op jit(solution)/shard_map/ppermute | solution.py:349
  115.4 11.5 %collective-permute-start.8 = (bf16[24,1024]{1,0:T(8,128)(2,1)}, bf16[24,1024]{1,0:T(8,128)(2,1)S(1)}, u32[]{:S(2)}, u32[]{:S(2)}) collective-permute-start(bf16[24,1024]{1,0:T(8,128)(2,1)} %get-tuple-element.31), channel_id=1, source_target_pairs={{0,3},{1,2},{2,1},{3,0},{4,7},{5,6},{6,5},{7,4},{8,11},{9,10},{10,... | collective-permute-start | bytes 147464 | tf_op jit(solution)/shard_map/ppermute | solution.py:349
  126.8 0.6 copy-start.6
  126.8 0.6 copy-start.7
  126.8 0.6 copy-start.8
Sparse Core Ops, SparseCore 0:
  13.8 34.0 all-gather.2
